TPU v7x, 256 devices: a whole 4x4x8 slice. The times are simulated.
256 devices in a mesh: hst: 16 (over z, y_lo), seq: 16 (over x, y_hi, core).
Axes of the slice: x: 4, y: 4 (y_hi: 2, y_lo: 2; y = y_hi * 2 + y_lo), z: 8, core: 2. Of those that a mesh axis runs over, the one named last changes fastest.
Arguments:
- queries: bfloat16 [16, 16, 2048, 128], P('hst', 'seq'), may hold values from -9 to 9
- keys: bfloat16 [16, 16, 2048, 128], P('hst', 'seq'), may hold values from -9 to 9
- values: bfloat16 [16, 16, 2048, 128], P('hst', 'seq'), may hold values from -6 to 6
- cotangent: bfloat16 [16, 2048, 3072], P('hst', 'seq'), may hold values from -6 to 6
- gate: float32 [16, 3072], P('hst'), may hold values from -4 to 4
- w_out: bfloat16 [2048, 3072], P('seq'), may hold values from -0.125 to 0.125
Outputs:
- grad_queries: bfloat16 [16, 16, 2048, 128], P('hst', 'seq')
- grad_keys: bfloat16 [16, 16, 2048, 128], P('hst', 'seq')
- grad_values: bfloat16 [16, 16, 2048, 128], P('hst', 'seq')
- grad_out_proj: float32 [2048, 3072], P('seq')
All inputs are finite; a program needn't handle non-finite values.
Results may differ from a plain program's by a relative error of at most 0.025.
Values may be sent and summed in bfloat16 or wider, within the bound.
No kernel may reach another device: no remote copies, remote signals or barrier semaphores. Data moves between devices by JAX's collectives and lax.ppermute only.
A program may use at most 128 MiB of HBM per device.

v0:
```python
import jax
import jax.numpy as jnp
from jax import lax
from jax.sharding import PartitionSpec as P


def contract_last(left, right):
    return lax.dot_general(
        left, right, (((1,), (1,)), ((), ())), preferred_element_type=jnp.float32
    )


def contract_first(left, right):
    return lax.dot_general(
        left, right, (((0,), (0,)), ((), ())), preferred_element_type=jnp.float32
    )


def shards(queries, keys, values, cotangent, gate, w_out):
    query_head = queries[0, 0]
    key_head = keys[0, 0]
    value_head = values[0, 0]
    seq_len, head_dim = query_head.shape
    scale = 1.0 / head_dim**0.5
    block = min(512, seq_len)
    block_count = seq_len // block
    gate_row = gate[0]

    def forward_block(index):
        rows = lax.dynamic_slice_in_dim(query_head, index * block, block, 0)
        scores = contract_last(rows, key_head) * scale
        row_max = jnp.max(scores, axis=-1, keepdims=True)
        log_total = row_max + jnp.log(jnp.sum(jnp.exp(scores - row_max), axis=-1, keepdims=True))
        probs = jnp.exp(scores - log_total)
        attn_rows = jnp.dot(
            probs.astype(jnp.bfloat16), value_head, preferred_element_type=jnp.float32
        )
        return (attn_rows.astype(jnp.bfloat16), log_total[:, 0])

    attn_blocks, log_blocks = lax.map(forward_block, jnp.arange(block_count))
    attn_head = attn_blocks.reshape(seq_len, head_dim)
    log_totals = log_blocks.reshape(seq_len)
    attn_tokens = lax.all_to_all(attn_head, "seq", split_axis=0, concat_axis=1, tiled=True)
    proj_local = (cotangent[0].astype(jnp.float32) * gate_row).astype(jnp.bfloat16)
    grad_tokens = contract_last(
        proj_local, lax.all_gather(w_out, "seq", axis=0, tiled=True)
    ).astype(jnp.bfloat16)
    grad_attn_head = lax.all_to_all(grad_tokens, "seq", split_axis=1, concat_axis=0, tiled=True)
    host_grad = lax.psum_scatter(
        contract_first(attn_tokens, proj_local).astype(jnp.bfloat16),
        "seq",
        scatter_dimension=0,
        tiled=True,
    )
    grad_out_proj = lax.psum(host_grad, "hst").astype(jnp.float32)

    def backward_block(carry, index):
        grad_key_sum, grad_value_sum = carry
        start = index * block
        rows = lax.dynamic_slice_in_dim(query_head, start, block, 0)
        grad_rows = lax.dynamic_slice_in_dim(grad_attn_head, start, block, 0)
        log_rows = lax.dynamic_slice_in_dim(log_totals, start, block, 0)
        scores = contract_last(rows, key_head) * scale
        probs = jnp.exp(scores - log_rows[:, None])
        probs16 = probs.astype(jnp.bfloat16)
        grad_probs = contract_last(grad_rows, value_head)
        delta = jnp.sum(probs * grad_probs, axis=-1, keepdims=True)
        grad_scores = (probs * (grad_probs - delta)).astype(jnp.bfloat16)
        grad_query_rows = (
            jnp.dot(grad_scores, key_head, preferred_element_type=jnp.float32) * scale
        ).astype(jnp.bfloat16)
        grad_key_sum = grad_key_sum + contract_first(grad_scores, rows)
        grad_value_sum = grad_value_sum + contract_first(probs16, grad_rows)
        return ((grad_key_sum, grad_value_sum), grad_query_rows)

    zeros_head = jnp.zeros((seq_len, head_dim), jnp.float32)
    sums, grad_query_blocks = lax.scan(
        backward_block, (zeros_head, zeros_head), jnp.arange(block_count)
    )
    grad_queries = grad_query_blocks.reshape(seq_len, head_dim)
    grad_keys = (sums[0] * scale).astype(jnp.bfloat16)
    grad_values = sums[1].astype(jnp.bfloat16)
    return (grad_queries[None, None], grad_keys[None, None], grad_values[None, None], grad_out_proj)


def solution(mesh):
    in_specs = (
        P("hst", "seq", None, None),
        P("hst", "seq", None, None),
        P("hst", "seq", None, None),
        P("hst", "seq", None),
        P("hst", None),
        P("seq", None),
    )
    out_specs = (
        P("hst", "seq", None, None),
        P("hst", "seq", None, None),
        P("hst", "seq", None, None),
        P("seq", None),
    )
    return jax.shard_map(shards, mesh=mesh, in_specs=in_specs, out_specs=out_specs, check_vma=False)
```

profile of v0, /device:TPU:2, one launch (start us, length us, event | category | flops | bytes accessed | tf_op | source)
XLA Modules:
  0.0 470.1 jit_solution(9265348245758362908)
XLA Ops:
  7.3 20.0 %while.27 = (s32[]{:T(128)}, bf16[4,512,128]{2,1,0:T(8,128)(2,1)S(1)}, f32[4,512]{1,0:T(4,128)S(1)}, s32[4]{0:T(128)S(1)}, bf16[2048,128]{1,0:T(8,128)(2,1)}, /*...) while((s32[]{:T(128)}, ...), condition=%wide.region_3.4_spmd, body=%wide.region_0.3_spmd.sunk | while | flops 545324544 | bytes 16009431 | solution.py:40
  8.6 2.0 multiply_reduce_fusion.4
  13.6 1.9 multiply_reduce_fusion.4
  18.6 1.9 multiply_reduce_fusion.4
  23.6 1.9 multiply_reduce_fusion.4
  27.4 17.3 %all_to_all.38 = bf16[16,128,128]{2,1,0:T(8,128)(2,1)S(1)} all-to-all(bf16[16,128,128]{2,1,0:T(8,128)(2,1)S(1)} %bitcast.80), channel_id=1, replica_groups=mesh['hst'=16,'seq'=16] {'seq'}, dimensions={0} | all-to-all | bytes 1048576 | tf_op jit(solution)/shard_map/all_to_all | solution.py:43
  44.9 6.4 %convolution_convert_fusion = bf16[2048,3072]{1,0:T(8,128)(2,1)} fusion(bf16[128,2048]{0,1:T(8,128)(2,1)S(1)} %bitcast.79, bf16[1,128,3072]{2,1,0:T(8,128)(2,1)S(1)} %copy-done.4, f32[3072]{0:T(1024)S(1)} %bitcast.84), kind=kOutput, calls=%fused_computation.33 | convolution fusion | flops 1618083840 | bytes 13905920 | tf_op jit(solution)/shard_map/dot_general | solution.py:14
  52.2 129.1 %reduce-scatter.2.cloned.1.call-done = bf16[128,3072]{1,0:T(8,128)(2,1)} async-done(((bf16[2048,3072]{1,0:T(8,128)(2,1)}), bf16[128,3072]{1,0:T(8,128)(2,1)}) %reduce-scatter.2.cloned.1.call-update) | async-done | bytes 786448 | tf_op jit(solution)/shard_map/reduce_scatter | solution.py:49
  181.3 96.9 %all-gather.2.cloned.1.call-done = bf16[2048,3072]{1,0:T(8,128)(2,1)} async-done(((bf16[128,3072]{1,0:T(8,128)(2,1)}), bf16[2048,3072]{1,0:T(8,128)(2,1)}) %all-gather.2.cloned.1.call-update) | async-done | bytes 12582928 | tf_op jit(solution)/shard_map/all_gather | solution.py:46
  278.1 8.8 %fusion.26 = bf16[16,16,8,128]{3,2,1,0:T(8,128)(2,1)S(1)} fusion(bf16[2048,3072]{1,0:T(8,128)(2,1)} %all-gather.2.cloned.1.call-done, bf16[1,128,3072]{2,1,0:T(8,128)(2,1)S(1)} %copy-done.4, f32[3072]{0:T(1024)S(1)} %bitcast.85), kind=kOutput, calls=%fused_computation.40 | convolution fusion | flops 1612054528 | bytes 13905920 | tf_op jit(solution)/shard_map/dot_general | solution.py:8
  288.0 5.8 %all-to-all-start = ((bf16[128,16,128]{2,0,1:T(8,128)(2,1)}), bf16[128,16,128]{2,0,1:T(8,128)(2,1)}, u32[]{:S(2)}, u32[]{:S(2)}) async-start(bf16[128,16,128]{2,0,1:T(8,128)(2,1)} %bitcast.51), calls=%async_computation | async-start | bytes 1048576 | tf_op jit(solution)/shard_map/all_to_all | solution.py:48
  293.8 127.4 %all-reduce.2.cloned.1.call-done = bf16[128,3072]{1,0:T(8,128)(2,1)} async-done(((bf16[128,3072]{1,0:T(8,128)(2,1)}), bf16[128,3072]{1,0:T(8,128)(2,1)}) %all-reduce.2.cloned.1.call-update) | async-done | bytes 786448 | tf_op jit(solution)/shard_map/psum | solution.py:55
  421.2 2.4 convert_element_type.57
  424.5 37.9 %while.28 = (s32[]{:T(128)}, f32[2048,128]{1,0:T(8,128)S(1)}, f32[2048,128]{1,0:T(8,128)S(1)}, bf16[4,512,128]{2,1,0:T(8,128)(2,1)}, s32[4]{0:T(128)S(1)}, /*ind...) while((s32[]{:T(128)}, f32[2048,128]{1,0:T(8,128)S(1)}, ...), condition=%wide.region_6.7_spmd.clone, body=%wide.region_4.6_spmd.clone.sunk | while | flops 1351745024 | bytes 39987460 | solution.py:77
  425.9 1.7 fusion.68
  429.3 2.2 convolution_add_fusion.5
  431.4 1.4 fusion.69
  435.3 1.7 fusion.68
  438.7 2.2 convolution_add_fusion.5
  444.8 1.7 fusion.68
  448.2 2.2 convolution_add_fusion.5
  454.3 1.7 fusion.68
  457.7 2.2 convolution_add_fusion.5
  459.9 1.4 fusion.69
  (84 shorter events, 30.7 us)
Async XLA Ops:
  7.2 174.1 %reduce-scatter.2.cloned.1.call-start = ((), (), s32[]{:S(2)}) async-start(), calls=%async_computation.4 | async-start | bytes 13369344 | tf_op jit(solution)/shard_map/reduce_scatter | solution.py:49
  7.3 37.6 %copy-start.4 = (bf16[1,128,3072]{2,1,0:T(8,128)(2,1)S(1)}, bf16[1,128,3072]{2,1,0:T(8,128)(2,1)}, u32[]{:S(2)}) copy-start(bf16[1,128,3072]{2,1,0:T(8,128)(2,1)} %param.13) | copy-start | bytes 2359300
  7.3 37.6 %copy-start.5 = (f32[1,3072]{1,0:T(1,128)S(1)}, f32[1,3072]{1,0:T(1,128)}, u32[]{:S(2)}) copy-start(f32[1,3072]{1,0:T(1,128)} %param.14) | copy-start | bytes 36868
  8.6 2.8 copy-start.1
  13.6 2.8 copy-start.1
  18.6 2.8 copy-start.1
  23.6 2.8 copy-start.1
  51.4 226.8 %all-gather.2.cloned.1.call-start = ((), (), s32[]{:S(2)}) async-start(), calls=%async_computation.3 | async-start | bytes 13369344 | tf_op jit(solution)/shard_map/all_gather | solution.py:46
  52.1 369.1 %all-reduce.2.cloned.1.call-start = ((), (), s32[]{:S(2)}) async-start(), calls=%async_computation.5 | async-start | bytes 1572864 | tf_op jit(solution)/shard_map/psum | solution.py:55
  287.0 137.5 %copy-start = (bf16[2048,128]{1,0:T(8,128)(2,1)S(1)}, bf16[2048,128]{1,0:T(8,128)(2,1)}, u32[]{:S(2)}) copy-start(bf16[2048,128]{1,0:T(8,128)(2,1)} %get-tuple-element.366) | copy-start | bytes 1572868
  287.0 137.5 %copy-start.2 = (bf16[2048,128]{1,0:T(8,128)(2,1)S(1)}, bf16[2048,128]{1,0:T(8,128)(2,1)}, u32[]{:S(2)}) copy-start(bf16[2048,128]{1,0:T(8,128)(2,1)} %get-tuple-element.367) | copy-start | bytes 1572868
  288.0 135.7 %all-to-all-start = ((bf16[128,16,128]{2,0,1:T(8,128)(2,1)}), bf16[128,16,128]{2,0,1:T(8,128)(2,1)}, u32[]{:S(2)}, u32[]{:S(2)}) async-start(bf16[128,16,128]{2,0,1:T(8,128)(2,1)} %bitcast.51), calls=%async_computation | async-start | bytes 1048576 | tf_op jit(solution)/shard_map/all_to_all | solution.py:48
  425.8 1.7 copy-start.3
  435.3 1.7 copy-start.3
  444.7 1.7 copy-start.3
  454.2 1.7 copy-start.3
Sparse Core Ops, SparseCore 0:
  51.5 129.7 reduce-scatter.1
  184.3 93.8 all-gather.1
  281.0 140.2 all-reduce.1
where the time goes:
time: 471 us; the launch traced here: 470 us
  waiting for transfers between devices  354 us (75%)
  matrix products  57.2 us (12%)
  blocking collectives  17.3 us (4%)
  between operations  13.9 us (3%)
  other arithmetic  8.64 us (2%)
  local copies, waits for them, and re-layouts  7.43 us (2%)
  starting transfers between devices  5.94 us (1%)
  loops' own time  5.63 us (1%)
    reduce_scatter x1, waiting for transfers between devices, shards(): lax.psum_scatter(contract_first(attn_tokens, proj_local).astype(jnp.bfloa...  129 us
    psum x1, waiting for transfers between devices, shards(): grad_out_proj = lax.psum(host_grad, 'hst').astype(jnp.float32)  127 us
    all_gather x1, waiting for transfers between devices, shards(): lax.all_gather(w_out, 'seq', axis=0, tiled=True)  96.9 us
    dot_general x13, matrix products, contract_last(): lax.dot_general(left, right, (((1,), (1,)), ((), ())), preferred_element_...  28.4 us
    dot_general x9, matrix products, contract_first(): lax.dot_general(left, right, (((0,), (0,)), ((), ())), preferred_element_...  19.7 us
    all_to_all x1, blocking collectives, shards(): lax.all_to_all(attn_head, 'seq', split_axis=0, concat_axis=1, tiled=True)  17.3 us
  transfers between devices with their start and end apart: 4, of which 3 were waited for; matrix products, arithmetic and copies ran while one was open for 3% of the time, Pallas kernels for 0%

commit v1 on v0

v1 whole, which is shorter than its diff:
```python
import functools

import jax
import jax.numpy as jnp
from jax import lax
from jax.experimental import pallas as pl
from jax.experimental.pallas import tpu as pltpu
from jax.sharding import PartitionSpec as P

AXES = ("hst", "seq")
LOG2E = 1.4426950408889634
CHUNKS = ((0, 1536), (1536, 3072))


def pairs(move):
    out = []
    for z in range(8):
        for y in range(4):
            for x in range(4):
                for core in range(2):
                    nx, ny, nc = move(x, y, core)
                    nx, ny = nx % 4, ny % 4
                    here = (z * 2 + y % 2) * 16 + x * 4 + (y // 2) * 2 + core
                    there = (z * 2 + ny % 2) * 16 + nx * 4 + (ny // 2) * 2 + nc
                    out.append((here, there))
    return out


FROM_X1 = pairs(lambda x, y, core: (x - 1, y, core))
FROM_X3 = pairs(lambda x, y, core: (x + 1, y, core))
FROM_X2 = pairs(lambda x, y, core: (x + 2, y, core))
SWAP_CORE = pairs(lambda x, y, core: (x, y, 1 - core))
SWAP_Y = pairs(lambda x, y, core: (x, y + 2, core))
MIRROR_Y = pairs(lambda x, y, core: (x, 3 - y, core))


def dot(left, right, left_dim, right_dim):
    return lax.dot_general(
        left, right, (((left_dim,), (right_dim,)), ((), ())), preferred_element_type=jnp.float32
    )


def forward_kernel(sub, scale, at_ref, q_ref, k_ref, v_ref, o_ref, inv_ref, p_ref):
    parts, _, rows, head_dim = q_ref.shape
    for part in range(parts):
        for start in range(0, rows, sub):
            here = pl.ds(part * rows + start, sub)
            scores = dot(q_ref[part, 0, pl.ds(start, sub), :], k_ref[...], 1, 1)
            row_max = jnp.max(scores, axis=1, keepdims=True)
            weights = jnp.exp2((scores - row_max) * (scale * LOG2E))
            inverse = 1.0 / jnp.sum(weights, axis=1, keepdims=True)
            weights16 = weights.astype(jnp.bfloat16)
            p_ref[here, :] = weights16
            o_ref[here, :] = (dot(weights16, v_ref[...], 1, 0) * inverse).astype(jnp.bfloat16)
            inv_ref[here, :] = jnp.broadcast_to(inverse, (sub, head_dim))


def forward_half(at, q4, keys, values):
    groups, _, rows, head_dim = q4.shape
    seq_len = keys.shape[0]
    half = groups * rows
    step = 2 * rows
    scale = 1.0 / head_dim**0.5
    block = lambda i, at: (i, 0)
    whole = lambda i, at: (0, 0)
    return pl.pallas_call(
        functools.partial(forward_kernel, 256, scale),
        grid_spec=pltpu.PrefetchScalarGridSpec(
            num_scalar_prefetch=1,
            grid=(groups // 2,),
            in_specs=[
                pl.BlockSpec((2, 1, rows, head_dim), lambda i, at: (i, at[0], 0, 0)),
                pl.BlockSpec((seq_len, head_dim), whole),
                pl.BlockSpec((seq_len, head_dim), whole),
            ],
            out_specs=[
                pl.BlockSpec((step, head_dim), block),
                pl.BlockSpec((step, head_dim), block),
                pl.BlockSpec((step, seq_len), block),
            ],
        ),
        out_shape=[
            jax.ShapeDtypeStruct((half, head_dim), jnp.bfloat16),
            jax.ShapeDtypeStruct((half, head_dim), jnp.float32),
            jax.ShapeDtypeStruct((half, seq_len), jnp.bfloat16),
        ],
        compiler_params=pltpu.CompilerParams(vmem_limit_bytes=30 << 20),
        cost_estimate=pl.CostEstimate(
            flops=5 * 10**9, bytes_accessed=6 << 20, transcendentals=half * seq_len
        ),
        name="attention_forward",
    )(at, q4, keys, values)


def backward_kernel(
    sub, scale, first, at_ref, q_ref, k_ref, v_ref, p_ref, g_ref, o_ref, inv_ref, *rest
):
    if first:
        dq_ref, dk_ref, dv_ref, dk_sum, dv_sum = rest
    else:
        dk_in, dv_in, _, dq_ref, dk_ref, dv_ref, dk_sum, dv_sum = rest
    step = pl.program_id(0)
    parts, _, rows, head_dim = q_ref.shape

    @pl.when(step == 0)
    def _():
        if first:
            dk_sum[...] = jnp.zeros_like(dk_sum)
            dv_sum[...] = jnp.zeros_like(dv_sum)
        else:
            dk_sum[...] = dk_in[...]
            dv_sum[...] = dv_in[...]

    for part in range(parts):
        for start in range(0, rows, sub):
            here = pl.ds(part * rows + start, sub)
            q_rows = q_ref[part, 0, pl.ds(start, sub), :]
            grad = g_ref[here, :].astype(jnp.float32) * inv_ref[here, :]
            grad16 = grad.astype(jnp.bfloat16)
            delta = jnp.sum(grad * o_ref[here, :].astype(jnp.float32), axis=1, keepdims=True)
            grad_probs = dot(grad16, v_ref[...], 1, 1)
            weights16 = p_ref[here, :]
            grad_scores = (weights16.astype(jnp.float32) * (grad_probs - delta)).astype(jnp.bfloat16)
            dq_ref[part, 0, pl.ds(start, sub), :] = (
                dot(grad_scores, k_ref[...], 1, 0) * scale
            ).astype(jnp.bfloat16)
            dk_sum[...] += dot(q_rows, grad_scores, 0, 0)
            dv_sum[...] += dot(grad16, weights16, 0, 0)

    @pl.when(step == pl.num_programs(0) - 1)
    def _():
        if first:
            dk_ref[...] = dk_sum[...]
            dv_ref[...] = dv_sum[...]
        else:
            dk_ref[...] = (dk_sum[...] * scale).T.astype(jnp.bfloat16)
            dv_ref[...] = dv_sum[...].T.astype(jnp.bfloat16)


def backward_half(at, q4, keys, values, weights, grad, attn, inverse, carry=None):
    groups, _, rows, head_dim = q4.shape
    seq_len = keys.shape[0]
    step = 2 * rows
    first = carry is None
    scale = 1.0 / head_dim**0.5
    block = lambda i, at: (i, 0)
    whole = lambda i, at: (0, 0)
    mine = pl.BlockSpec((2, 1, rows, head_dim), lambda i, at: (i, at[0], 0, 0))
    full = pl.BlockSpec((seq_len, head_dim), whole)
    flat = pl.BlockSpec((head_dim, seq_len), whole)
    rows_spec = pl.BlockSpec((step, head_dim), block)
    in_specs = [
        mine,
        full,
        full,
        pl.BlockSpec((step, seq_len), block),
        rows_spec,
        rows_spec,
        rows_spec,
    ]
    operands = [at, q4, keys, values, weights, grad, attn, inverse]
    dq_shape = jax.ShapeDtypeStruct(q4.shape, jnp.bfloat16)
    if first:
        out_specs = [mine, flat, flat]
        sums = jax.ShapeDtypeStruct((head_dim, seq_len), jnp.float32)
        aliases = {}
    else:
        in_specs += [flat, flat, pl.BlockSpec(memory_space=pl.ANY)]
        operands += [carry[1], carry[2], carry[0]]
        out_specs = [mine, full, full]
        sums = jax.ShapeDtypeStruct((seq_len, head_dim), jnp.bfloat16)
        aliases = {len(operands) - 1: 0}
    return pl.pallas_call(
        functools.partial(backward_kernel, 256, scale, first),
        grid_spec=pltpu.PrefetchScalarGridSpec(
            num_scalar_prefetch=1,
            grid=(groups // 2,),
            in_specs=in_specs,
            out_specs=out_specs,
            scratch_shapes=[
                pltpu.VMEM((head_dim, seq_len), jnp.float32),
                pltpu.VMEM((head_dim, seq_len), jnp.float32),
            ],
        ),
        out_shape=[dq_shape, sums, sums],
        input_output_aliases=aliases,
        compiler_params=pltpu.CompilerParams(vmem_limit_bytes=36 << 20),
        cost_estimate=pl.CostEstimate(flops=6 * 10**9, bytes_accessed=8 << 20, transcendentals=0),
        name="attention_backward",
    )(*operands)


def projection_kernel(place_ref, own_ref, other_ref, gate_ref, *refs):
    blocks, (own_out, other_out) = refs[:-2], refs[-2:]
    size = blocks[0].shape[0]
    tokens = jnp.concatenate([block[...] for block in blocks], axis=0)

    def rows(ref):
        return jnp.concatenate(
            [
                ref[pl.ds(pl.multiple_of(place_ref[slot] * size, size), size), :]
                for slot in range(len(blocks))
            ],
            axis=0,
        )

    gate = gate_ref[...]
    other_out[...] = (dot(rows(other_ref), tokens, 0, 0) * gate).astype(jnp.bfloat16)
    own_out[...] = (dot(rows(own_ref), tokens, 0, 0) * gate).astype(jnp.bfloat16)


def projection_grad(place, attn_own, attn_other, gate, blocks, tile=512):
    size, columns = blocks[0].shape
    half, head_dim = attn_own.shape
    tile = min(tile, columns)
    column = lambda i, place: (0, i)
    whole = pl.BlockSpec((half, head_dim), lambda i, place: (0, 0))
    out = jax.ShapeDtypeStruct((head_dim, columns), jnp.bfloat16)
    return pl.pallas_call(
        projection_kernel,
        grid_spec=pltpu.PrefetchScalarGridSpec(
            num_scalar_prefetch=1,
            grid=(columns // tile,),
            in_specs=[whole, whole, pl.BlockSpec((1, tile), column)]
            + [pl.BlockSpec((size, tile), column)] * len(blocks),
            out_specs=[pl.BlockSpec((head_dim, tile), column)] * 2,
        ),
        out_shape=[out, out],
        compiler_params=pltpu.CompilerParams(vmem_limit_bytes=24 << 20),
        cost_estimate=pl.CostEstimate(
            flops=4 * half * head_dim * columns, bytes_accessed=half * columns * 2, transcendentals=0
        ),
        name="projection_grad",
    )(place, attn_own, attn_other, gate, *blocks)


def tokens_kernel(counts, place_ref, weight_ref, *refs):
    blocks, (own_out, other_out, total) = refs[:-3], refs[-3:]
    step = pl.program_id(0)
    slots = len(blocks) // len(counts)
    size = blocks[0].shape[0]
    head_dim = own_out.shape[1]

    @pl.when(step == 0)
    def _():
        total[...] = jnp.zeros_like(total)

    start = 0
    for index, count in enumerate(counts):
        group = blocks[index * slots : (index + 1) * slots]

        @pl.when((step >= start) & (step < start + count))
        def _(group=group):
            tokens = jnp.concatenate([block[...] for block in group], axis=0)
            total[...] += dot(tokens, weight_ref[...], 1, 1)

        start += count

    @pl.when(step == pl.num_programs(0) - 1)
    def _():
        for slot in range(slots):
            here = pl.ds(pl.multiple_of(place_ref[slot] * size, size), size)
            rows = total[pl.ds(slot * size, size), :]
            own_out[here, :] = rows[:, :head_dim].astype(jnp.bfloat16)
            other_out[here, :] = rows[:, head_dim:].astype(jnp.bfloat16)


def tokens_grad(place, weight, groups, tile=512):
    size = groups[0][0].shape[0]
    slots = len(groups[0])
    heads = weight.shape[0]
    counts = [group[0].shape[1] // tile for group in groups]
    specs, blocks, start = [], [], 0
    for group, count in zip(groups, counts):
        index = lambda i, place, start=start, count=count: (0, jnp.clip(i - start, 0, count - 1))
        specs += [pl.BlockSpec((size, tile), index)] * slots
        blocks += list(group)
        start += count
    half = slots * size
    out = jax.ShapeDtypeStruct((half, heads // 2), jnp.bfloat16)
    whole = pl.BlockSpec((half, heads // 2), lambda i, place: (0, 0))
    return pl.pallas_call(
        functools.partial(tokens_kernel, counts),
        grid_spec=pltpu.PrefetchScalarGridSpec(
            num_scalar_prefetch=1,
            grid=(start,),
            in_specs=[pl.BlockSpec((heads, tile), lambda i, place: (0, i))] + specs,
            out_specs=[whole, whole],
            scratch_shapes=[pltpu.VMEM((half, heads), jnp.float32)],
        ),
        out_shape=[out, out],
        compiler_params=pltpu.CompilerParams(vmem_limit_bytes=30 << 20),
        cost_estimate=pl.CostEstimate(
            flops=2 * half * heads * tile * start, bytes_accessed=8 << 20, transcendentals=0
        ),
        name="tokens_grad",
    )(place, weight, *blocks)


def send(array, perm):
    return lax.ppermute(array, AXES, perm)


def shards(queries, keys, values, cotangent, gate, w_out):
    query_head, key_head, value_head = queries[0, 0], keys[0, 0], values[0, 0]
    seq_len, head_dim = query_head.shape
    seq = lax.axis_index("seq")
    x, y_hi, core = seq // 4, (seq // 2) % 2, seq % 2
    mine = jnp.reshape(y_hi, (1,)).astype(jnp.int32)
    theirs = 1 - mine
    place = jnp.stack(
        [((x + dx) % 4) * 2 + (core ^ e) for dx in range(4) for e in range(2)]
    ).astype(jnp.int32)
    q4 = query_head.reshape(4, 2, seq_len // 8, head_dim)

    groups = []
    for low, high in CHUNKS:
        block = cotangent[0][:, low:high]
        own = [block, send(block, FROM_X1), send(block, FROM_X2), send(block, FROM_X3)]
        groups.append([part for piece in own for part in (piece, send(piece, SWAP_CORE))])
    w_other = send(w_out, MIRROR_Y)
    weight = jnp.concatenate(
        [(w.astype(jnp.float32) * gate).astype(jnp.bfloat16) for w in (w_out, w_other)], axis=0
    )

    attn_theirs, inv_theirs, p_theirs = forward_half(theirs, q4, key_head, value_head)
    attn_other = send(attn_theirs, SWAP_Y)
    attn_mine, inv_mine, p_mine = forward_half(mine, q4, key_head, value_head)

    outs = []
    for (low, high), group in zip(CHUNKS, groups):
        own, other = projection_grad(place, attn_mine, attn_other, gate[:, low:high], group)
        columns = high - low
        summed = own.astype(jnp.float32) + send(other, SWAP_Y).astype(jnp.float32)
        pieces = summed.astype(jnp.bfloat16).reshape(16, head_dim // 16, columns)
        pieces = lax.all_to_all(pieces, "hst", 0, 0, tiled=True)
        piece = jnp.sum(pieces.astype(jnp.float32), axis=0).astype(jnp.bfloat16)
        everywhere = lax.all_to_all(
            jnp.broadcast_to(piece[None], (16,) + piece.shape), "hst", 0, 0, tiled=True
        )
        outs.append(everywhere.reshape(head_dim, columns).astype(jnp.float32))
    grad_out_proj = jnp.concatenate(outs, axis=1)

    grad_mine, grad_other = tokens_grad(place, weight, groups)
    grad_theirs = send(grad_other, SWAP_Y)
    carry = backward_half(
        mine, q4, key_head, value_head, p_mine, grad_mine, attn_mine, inv_mine
    )
    dq, dk, dv = backward_half(
        theirs, q4, key_head, value_head, p_theirs, grad_theirs, attn_theirs, inv_theirs, carry
    )
    return (
        dq.reshape(1, 1, seq_len, head_dim),
        dk[None, None],
        dv[None, None],
        grad_out_proj,
    )


def solution(mesh):
    in_specs = (
        P("hst", "seq", None, None),
        P("hst", "seq", None, None),
        P("hst", "seq", None, None),
        P("hst", "seq", None),
        P("hst", None),
        P("seq", None),
    )
    out_specs = (
        P("hst", "seq", None, None),
        P("hst", "seq", None, None),
        P("hst", "seq", None, None),
        P("seq", None),
    )
    return jax.shard_map(shards, mesh=mesh, in_specs=in_specs, out_specs=out_specs, check_vma=False)
```

time: 471 us -> 154 us (0.33)
  waiting for transfers between devices: 354 us -> 43.1 us
  matrix products: 57.2 us -> 0 us
  starting transfers between devices: 5.94 us -> 48.1 us
  Pallas kernels: 0 us -> 29.5 us
  blocking collectives: 17.3 us -> 0 us
  local copies, waits for them, and re-layouts: 7.43 us -> 20.6 us
  between operations: 13.9 us -> 1.04 us
  loops' own time: 5.63 us -> 0 us
    reduce_scatter x1 -> x0, waiting for transfers between devices: 129 us -> none  [shards(): lax.psum_scatter(contract_first(attn_tokens, proj_local).astype(jnp.bfloa...]
    psum x1 -> x0, waiting for transfers between devices: 127 us -> none  [shards(): grad_out_proj = lax.psum(host_grad, 'hst').astype(jnp.float32)]
    all_gather x1 -> x0, waiting for transfers between devices: 96.9 us -> none  [shards(): lax.all_gather(w_out, 'seq', axis=0, tiled=True)]
    dot_general x30 -> x0, matrix products: 57.2 us -> none  [the longest x13 28.4 us: contract_last(): lax.dot_general(left, right, (((1,), (1,)), ((), ())), preferred_element_...]
    pallas_call x0 -> x7, Pallas kernels: none -> 29.5 us  [the longest x2 10.8 us: backward_half(): pl.pallas_call(functools.partial(backward_kernel, 256, scale, first), gri...]
    ppermute x0 -> x19, starting transfers between devices: none -> 23.5 us  [send(): return lax.ppermute(array, AXES, perm)]
    ppermute x0 -> x19, waiting for transfers between devices: none -> 23.3 us  [send(): return lax.ppermute(array, AXES, perm)]
    all_to_all x1 -> x4, waiting for transfers between devices: 0.01 us -> 19.9 us  [the longest x2 19.9 us: shards(): pieces = lax.all_to_all(pieces, 'hst', 0, 0, tiled=True)]
  transfers between devices with their start and end apart: 4 -> 23, of which waited for: 3 -> 9; matrix products, arithmetic and copies ran while one was open for 3% -> 6% of each run, Pallas kernels for 0% -> 17%
where the time goes in v1:
time: 154 us; the launch traced here: 152 us
  starting transfers between devices  48.1 us (31%)
  waiting for transfers between devices  43.1 us (28%)
  Pallas kernels  29.5 us (19%)
  local copies, waits for them, and re-layouts  20.6 us (13%)
  other arithmetic  9.66 us (6%)
    ppermute x19, starting transfers between devices, send(): return lax.ppermute(array, AXES, perm)  23.5 us
    ppermute x19, waiting for transfers between devices, send(): return lax.ppermute(array, AXES, perm)  23.3 us
    all_to_all x2, waiting for transfers between devices, shards(): pieces = lax.all_to_all(pieces, 'hst', 0, 0, tiled=True)  19.9 us
    unnamed x84, local copies, waits for them, and re-layouts  18.2 us
    all_to_all x2, starting transfers between devices, shards(): pieces = lax.all_to_all(pieces, 'hst', 0, 0, tiled=True)  12.9 us
    all_to_all x2, starting transfers between devices, shards(): lax.all_to_all(jnp.broadcast_to(piece[None], (16,) + piece.shape), 'hst',...  11.6 us
    pallas_call x2, Pallas kernels, backward_half(): pl.pallas_call(functools.partial(backward_kernel, 256, scale, first), gri...  10.8 us
    pallas_call x2, Pallas kernels, forward_half(): pl.pallas_call(functools.partial(forward_kernel, 256, scale), grid_spec=p...  7.66 us
  transfers between devices with their start and end apart: 23, of which 9 were waited for; matrix products, arithmetic and copies ran while one was open for 6% of the time, Pallas kernels for 17%

profile of v1, /device:TPU:2, one launch (start us, length us, event | category | flops | bytes accessed | tf_op | source)
XLA Modules:
  0.0 152.1 jit_solution(17138572783435734949)
XLA Ops:
  3.8 3.8 %attention_forward.2 = (bf16[1024,128]{1,0:T(8,128)(2,1)S(1)}, f32[1024,128]{1,0:T(8,128)S(1)}, bf16[1024,2048]{1,0:T(8,128)(2,1)S(1)}) custom-call(s32[1]{0:T(128)S(6)} %sub.11.at_ref, bf16[4,2,256,128]{3,2,1,0:T(8,128)(2,1)S(1)} %bitcast.23, bf16[2048,128]{1,0:T(8,128)(2,1)S(1)} %bitcast.27, bf16[2048,128]{1,0:T(8,128)(2,1)S(1)} %bitcast.31), custom_call_target="tpu_custom_call" | custom-call | flops 5000000000 | bytes 6291456 | tf_op jit(solution)/shard_map/attention_forward/pallas_call | solution.py:66
  9.6 3.2 %collective-permute-start.16 = (bf16[1024,128]{1,0:T(8,128)(2,1)S(1)}, bf16[1024,128]{1,0:T(8,128)(2,1)S(1)}, u32[]{:S(2)}, u32[]{:S(2)}) collective-permute-start(bf16[1024,128]{1,0:T(8,128)(2,1)S(1)} %get-tuple-element.24.o_ref), channel_id=1, source_target_pairs={{0,2},{1,3},{4,6},{5,7},{8,10},{9,11},{12,14},{13,15},{16,18},{17,... | collective-permute-start | bytes 786440 | tf_op jit(solution)/shard_map/ppermute | solution.py:301
  23.5 3.8 %attention_forward.3 = (bf16[1024,128]{1,0:T(8,128)(2,1)S(1)}, f32[1024,128]{1,0:T(8,128)S(1)}, bf16[1024,2048]{1,0:T(8,128)(2,1)S(1)}) custom-call(s32[1]{0:T(128)} %bitcast.at_ref, bf16[4,2,256,128]{3,2,1,0:T(8,128)(2,1)S(1)} %bitcast.24, bf16[2048,128]{1,0:T(8,128)(2,1)S(1)} %bitcast.28, bf16[2048,128]{1,0:T(8,128)(2,1)S(1)} %bitcast.32), custom_call_target="tpu_custom_call" | custom-call | flops 5000000000 | bytes 6291456 | tf_op jit(solution)/shard_map/attention_forward/pallas_call | solution.py:66
  29.3 2.6 %collective-permute-done.13.refs_14_.refs_6_ = bf16[128,1536]{1,0:T(8,128)(2,1)S(1)} collective-permute-done((bf16[128,1536]{1,0:T(8,128)(2,1)S(1)}, bf16[128,1536]{1,0:T(8,128)(2,1)S(1)}, u32[]{:S(2)}, u32[]{:S(2)}) %collective-permute-start.13) | collective-permute-done | bytes 393248 | tf_op jit(solution)/shard_map/ppermute | solution.py:301
  31.9 5.0 %collective-permute-start.2 = (bf16[128,1536]{1,0:T(8,128)(2,1)S(1)}, bf16[128,1536]{1,0:T(8,128)(2,1)S(1)}, u32[]{:S(2)}, u32[]{:S(2)}) collective-permute-start(bf16[128,1536]{1,0:T(8,128)(2,1)S(1)} %get-tuple-element.41.refs_0_), channel_id=1, source_target_pairs={{0,12},{1,13},{4,0},{5,1},{8,4},{9,5},{12,8},{13,9},{16,28},{17,29... | collective-permute-start | bytes 1179656 | tf_op jit(solution)/shard_map/ppermute | solution.py:301
  37.0 4.1 %collective-permute-done.9.refs_10_.refs_2_ = bf16[128,1536]{1,0:T(8,128)(2,1)S(1)} collective-permute-done((bf16[128,1536]{1,0:T(8,128)(2,1)S(1)}, bf16[128,1536]{1,0:T(8,128)(2,1)S(1)}, u32[]{:S(2)}, u32[]{:S(2)}) %collective-permute-start.9) | collective-permute-done | bytes 393248 | tf_op jit(solution)/shard_map/ppermute | solution.py:301
  41.9 3.6 %collective-permute-done.4.refs_4_ = bf16[128,1536]{1,0:T(8,128)(2,1)S(1)} collective-permute-done((bf16[128,1536]{1,0:T(8,128)(2,1)S(1)}, bf16[128,1536]{1,0:T(8,128)(2,1)S(1)}, u32[]{:S(2)}, u32[]{:S(2)}) %collective-permute-start.4) | collective-permute-done | bytes 393248 | tf_op jit(solution)/shard_map/ppermute | solution.py:301
  45.5 5.3 %collective-permute-done.2.refs_2_ = bf16[128,1536]{1,0:T(8,128)(2,1)S(1)} collective-permute-done((bf16[128,1536]{1,0:T(8,128)(2,1)S(1)}, bf16[128,1536]{1,0:T(8,128)(2,1)S(1)}, u32[]{:S(2)}, u32[]{:S(2)}) %collective-permute-start.2) | collective-permute-done | bytes 393248 | tf_op jit(solution)/shard_map/ppermute | solution.py:301
  51.6 2.5 %projection_grad.3 = (bf16[128,1536]{1,0:T(8,128)(2,1)S(1)}, bf16[128,1536]{1,0:T(8,128)(2,1)S(1)}) custom-call(s32[8]{0:T(128)S(1)} %stack.35.place_ref, bf16[1024,128]{1,0:T(8,128)(2,1)S(1)} %get-tuple-element.28.o_ref.own_ref, bf16[1024,128]{1,0:T(8,128)(2,1)S(1)} %copy-done.15, f32[1,1536]{1,0:T(1,128)S(1)} %get-tuple-element.43.gate_ref, ...), custom_call_target="tpu_custom_call" | custom-call | flops 805306368 | bytes 3145728 | tf_op jit(solution)/shard_map/projection_grad/pallas_call | solution.py:219
  55.0 3.1 %projection_grad.2 = (bf16[128,1536]{1,0:T(8,128)(2,1)S(1)}, bf16[128,1536]{1,0:T(8,128)(2,1)}) custom-call(s32[8]{0:T(128)S(1)} %stack.35.place_ref, bf16[1024,128]{1,0:T(8,128)(2,1)S(1)} %get-tuple-element.28.o_ref.own_ref, bf16[1024,128]{1,0:T(8,128)(2,1)S(1)} %copy-done.15, f32[1,1536]{1,0:T(1,128)S(1)} %get-tuple-element.42.gate_ref, ...), custom_call_target="tpu_custom_call" | custom-call | flops 805306368 | bytes 3145728 | tf_op jit(solution)/shard_map/projection_grad/pallas_call | solution.py:219
  59.0 2.8 %collective-permute-start.17 = (bf16[128,1536]{1,0:T(8,128)(2,1)}, bf16[128,1536]{1,0:T(8,128)(2,1)}, u32[]{:S(2)}, u32[]{:S(2)}) collective-permute-start(bf16[128,1536]{1,0:T(8,128)(2,1)} %get-tuple-element.37), channel_id=1, source_target_pairs={{0,2},{1,3},{4,6},{5,7},{8,10},{9,11},{12,14},{13,15},{16,18},{17,... | collective-permute-start | bytes 1179656 | tf_op jit(solution)/shard_map/ppermute | solution.py:301
  61.8 5.9 %collective-permute-done.18 = bf16[128,1536]{1,0:T(8,128)(2,1)S(1)} collective-permute-done((bf16[128,1536]{1,0:T(8,128)(2,1)S(1)}, bf16[128,1536]{1,0:T(8,128)(2,1)S(1)}, u32[]{:S(2)}, u32[]{:S(2)}) %collective-permute-start.18) | collective-permute-done | bytes 393248 | tf_op jit(solution)/shard_map/ppermute | solution.py:301
  68.6 8.7 %all-to-all-start.2 = ((bf16[16,8,1536]{2,1,0:T(8,128)(2,1)}), bf16[16,8,1536]{2,1,0:T(8,128)(2,1)}, u32[]{:S(2)}, u32[]{:S(2)}) async-start(bf16[16,8,1536]{2,1,0:T(8,128)(2,1)} %fusion.1), calls=%async_computation.2 | async-start | bytes 786432 | tf_op jit(solution)/shard_map/all_to_all | solution.py:336
  77.3 2.2 %collective-permute-start = (bf16[128,3072]{1,0:T(8,128)(2,1)}, bf16[128,3072]{1,0:T(8,128)(2,1)}, u32[]{:S(2)}, u32[]{:S(2)}) collective-permute-start(bf16[128,3072]{1,0:T(8,128)(2,1)} %param.11), channel_id=1, source_target_pairs={{0,18},{1,19},{4,22},{5,23},{8,26},{9,27},{12,30},{13,31},{16,2},{... | collective-permute-start | bytes 2359304 | tf_op jit(solution)/shard_map/ppermute | solution.py:301
  81.5 9.4 %all-to-all-done.2 = bf16[16,8,1536]{2,1,0:T(8,128)(2,1)} async-done(((bf16[16,8,1536]{2,1,0:T(8,128)(2,1)}), bf16[16,8,1536]{2,1,0:T(8,128)(2,1)}, u32[]{:S(2)}, u32[]{:S(2)}) %all-to-all-start.2) | async-done | bytes 393248 | tf_op jit(solution)/shard_map/all_to_all | solution.py:336
  90.9 4.2 %all-to-all-start = ((bf16[16,8,1536]{2,1,0:T(8,128)(2,1)}), bf16[16,8,1536]{2,1,0:T(8,128)(2,1)}, u32[]{:S(2)}, u32[]{:S(2)}) async-start(bf16[16,8,1536]{2,1,0:T(8,128)(2,1)} %fusion), calls=%async_computation | async-start | bytes 786432 | tf_op jit(solution)/shard_map/all_to_all | solution.py:336
  96.8 10.5 %all-to-all-done = bf16[16,8,1536]{2,1,0:T(8,128)(2,1)} async-done(((bf16[16,8,1536]{2,1,0:T(8,128)(2,1)}), bf16[16,8,1536]{2,1,0:T(8,128)(2,1)}, u32[]{:S(2)}, u32[]{:S(2)}) %all-to-all-start) | async-done | bytes 393248 | tf_op jit(solution)/shard_map/all_to_all | solution.py:336
  108.8 4.2 %all-to-all-start.3 = ((bf16[16,8,1536]{2,1,0:T(8,128)(2,1)}), bf16[16,8,1536]{2,1,0:T(8,128)(2,1)}, u32[]{:S(2)}, u32[]{:S(2)}) async-start(bf16[16,8,1536]{2,1,0:T(8,128)(2,1)} %broadcast_in_dim.21), calls=%async_computation.3 | async-start | bytes 786432 | tf_op jit(solution)/shard_map/all_to_all | solution.py:338
  116.5 5.5 %tokens_grad.1 = (bf16[1024,128]{1,0:T(8,128)(2,1)S(1)}, bf16[1024,128]{1,0:T(8,128)(2,1)}) custom-call(s32[8]{0:T(128)S(1)} %stack.35.place_ref, bf16[256,3072]{1,0:T(8,128)(2,1)S(1)} %pad_maximum_fusion.weight_ref, bf16[128,1536]{1,0:T(8,128)(2,1)S(1)} %get-tuple-element.41.refs_0_, bf16[128,1536]{1,0:T(8,128)(2,1)S(1)} %copy-done.7, ...), custom_call_target="tpu_custom_call" | custom-call | flops 1610612736 | bytes 8388608 | tf_op jit(solution)/shard_map/tokens_grad/pallas_call | solution.py:282
  126.3 7.4 %all-to-all-start.1 = ((bf16[16,8,1536]{2,1,0:T(8,128)(2,1)}), bf16[16,8,1536]{2,1,0:T(8,128)(2,1)S(1)}, u32[]{:S(2)}, u32[]{:S(2)}) async-start(bf16[16,8,1536]{2,1,0:T(8,128)(2,1)} %broadcast_in_dim.20), calls=%async_computation.1 | async-start | bytes 786432 | tf_op jit(solution)/shard_map/all_to_all | solution.py:338
  135.7 2.2 %copy-done.35 = bf16[1024,2048]{1,0:T(8,128)(2,1)S(1)} copy-done((bf16[1024,2048]{1,0:T(8,128)(2,1)S(1)}, bf16[1024,2048]{1,0:T(8,128)(2,1)}, u32[]{:S(2)}) %copy-start.35) | copy-done | bytes 4194328
  139.0 4.6 %attention_backward.2 = (bf16[4,2,256,128]{3,2,1,0:T(8,128)(2,1)}, f32[128,2048]{1,0:T(8,128)S(1)}, f32[128,2048]{1,0:T(8,128)S(1)}) custom-call(s32[1]{0:T(128)} %bitcast.at_ref, bf16[4,2,256,128]{3,2,1,0:T(8,128)(2,1)S(1)} %bitcast.25, bf16[2048,128]{1,0:T(8,128)(2,1)S(1)} %bitcast.29, bf16[2048,128]{1,0:T(8,128)(2,1)S(1)} %bitcast.33, ...), custom_call_target="tpu_custom_call" | custom-call | flops 6000000000 | bytes 8388608 | tf_op jit(solution)/shard_map/attention_backward/pallas_call | solution.py:173
  143.6 6.2 %attention_backward.3 = (bf16[4,2,256,128]{3,2,1,0:T(8,128)(2,1)}, bf16[2048,128]{1,0:T(8,128)(2,1)}, bf16[2048,128]{1,0:T(8,128)(2,1)}) custom-call(s32[1]{0:T(128)S(6)} %sub.11.at_ref, bf16[4,2,256,128]{3,2,1,0:T(8,128)(2,1)S(1)} %bitcast.26, bf16[2048,128]{1,0:T(8,128)(2,1)S(1)} %bitcast.30, ...), custom_call_target="tpu_custom_call", output_to_operand_aliasing={{0}: (10, {})} | custom-call | flops 6000000000 | bytes 8388608 | tf_op jit(solution)/shard_map/attention_backward/pallas_call | solution.py:173
  149.8 2.3 %maximum_convert_fusion = f32[128,3072]{1,0:T(8,128)} fusion(bf16[128,1536]{1,0:T(8,128)(2,1)} %bitcast.20, bf16[128,1536]{1,0:T(8,128)(2,1)S(1)} %bitcast.35), kind=kLoop, calls=%fused_computation.3 | loop fusion | flops 1572864 | bytes 2359296 | tf_op jit(solution)/shard_map/concatenate | solution.py:342
  (125 shorter events, 37.9 us)
Async XLA Ops:
  9.6 9.6 %collective-permute-start.16 = (bf16[1024,128]{1,0:T(8,128)(2,1)S(1)}, bf16[1024,128]{1,0:T(8,128)(2,1)S(1)}, u32[]{:S(2)}, u32[]{:S(2)}) collective-permute-start(bf16[1024,128]{1,0:T(8,128)(2,1)S(1)} %get-tuple-element.24.o_ref), channel_id=1, source_target_pairs={{0,2},{1,3},{4,6},{5,7},{8,10},{9,11},{12,14},{13,15},{16,18},{17,... | collective-permute-start | bytes 786440 | tf_op jit(solution)/shard_map/ppermute | solution.py:301
  12.9 19.0 %collective-permute-start.13 = (bf16[128,1536]{1,0:T(8,128)(2,1)S(1)}, bf16[128,1536]{1,0:T(8,128)(2,1)S(1)}, u32[]{:S(2)}, u32[]{:S(2)}) collective-permute-start(bf16[128,1536]{1,0:T(8,128)(2,1)S(1)} %get-tuple-element.40.refs_8_.refs_0_), channel_id=1, source_target_pairs={{0,4},{1,5},{4,8},{5,9},{8,12},{9,13},{12,0},{13,1},{16,20},{17,21... | collective-permute-start | bytes 1179656 | tf_op jit(solution)/shard_map/ppermute | solution.py:301
  14.4 17.5 %collective-permute-start.11 = (bf16[128,1536]{1,0:T(8,128)(2,1)S(1)}, bf16[128,1536]{1,0:T(8,128)(2,1)S(1)}, u32[]{:S(2)}, u32[]{:S(2)}) collective-permute-start(bf16[128,1536]{1,0:T(8,128)(2,1)S(1)} %get-tuple-element.40.refs_8_.refs_0_), channel_id=1, source_target_pairs={{0,8},{1,9},{4,12},{5,13},{8,0},{9,1},{12,4},{13,5},{16,24},{17,25... | collective-permute-start | bytes 1179656 | tf_op jit(solution)/shard_map/ppermute | solution.py:301
  15.6 25.4 %collective-permute-start.9 = (bf16[128,1536]{1,0:T(8,128)(2,1)S(1)}, bf16[128,1536]{1,0:T(8,128)(2,1)S(1)}, u32[]{:S(2)}, u32[]{:S(2)}) collective-permute-start(bf16[128,1536]{1,0:T(8,128)(2,1)S(1)} %get-tuple-element.40.refs_8_.refs_0_), channel_id=1, source_target_pairs={{0,12},{1,13},{4,0},{5,1},{8,4},{9,5},{12,8},{13,9},{16,28},{17,29... | collective-permute-start | bytes 1179656 | tf_op jit(solution)/shard_map/ppermute | solution.py:301
  17.7 23.3 %collective-permute-start.8 = (bf16[128,1536]{1,0:T(8,128)(2,1)S(1)}, bf16[128,1536]{1,0:T(8,128)(2,1)S(1)}, u32[]{:S(2)}, u32[]{:S(2)}) collective-permute-start(bf16[128,1536]{1,0:T(8,128)(2,1)S(1)} %get-tuple-element.40.refs_8_.refs_0_), channel_id=1, source_target_pairs={{0,1},{1,0},{4,5},{5,4},{8,9},{9,8},{12,13},{13,12},{16,17},{17,16... | collective-permute-start | bytes 1179656 | tf_op jit(solution)/shard_map/ppermute | solution.py:301
  19.9 31.8 %copy-start.15 = (bf16[1024,128]{1,0:T(8,128)(2,1)S(1)}, bf16[1024,128]{1,0:T(8,128)(2,1)}, u32[]{:S(2)}) copy-start(bf16[1024,128]{1,0:T(8,128)(2,1)} %copy-done.14) | copy-start | bytes 786436
  19.9 22.0 %collective-permute-start.6 = (bf16[128,1536]{1,0:T(8,128)(2,1)S(1)}, bf16[128,1536]{1,0:T(8,128)(2,1)S(1)}, u32[]{:S(2)}, u32[]{:S(2)}) collective-permute-start(bf16[128,1536]{1,0:T(8,128)(2,1)S(1)} %get-tuple-element.41.refs_0_), channel_id=1, source_target_pairs={{0,4},{1,5},{4,8},{5,9},{8,12},{9,13},{12,0},{13,1},{16,20},{17,21... | collective-permute-start | bytes 1179656 | tf_op jit(solution)/shard_map/ppermute | solution.py:301
  31.9 13.6 %collective-permute-start.4 = (bf16[128,1536]{1,0:T(8,128)(2,1)S(1)}, bf16[128,1536]{1,0:T(8,128)(2,1)S(1)}, u32[]{:S(2)}, u32[]{:S(2)}) collective-permute-start(bf16[128,1536]{1,0:T(8,128)(2,1)S(1)} %get-tuple-element.41.refs_0_), channel_id=1, source_target_pairs={{0,8},{1,9},{4,12},{5,13},{8,0},{9,1},{12,4},{13,5},{16,24},{17,25... | collective-permute-start | bytes 1179656 | tf_op jit(solution)/shard_map/ppermute | solution.py:301
  31.9 18.9 %collective-permute-start.2 = (bf16[128,1536]{1,0:T(8,128)(2,1)S(1)}, bf16[128,1536]{1,0:T(8,128)(2,1)S(1)}, u32[]{:S(2)}, u32[]{:S(2)}) collective-permute-start(bf16[128,1536]{1,0:T(8,128)(2,1)S(1)} %get-tuple-element.41.refs_0_), channel_id=1, source_target_pairs={{0,12},{1,13},{4,0},{5,1},{8,4},{9,5},{12,8},{13,9},{16,28},{17,29... | collective-permute-start | bytes 1179656 | tf_op jit(solution)/shard_map/ppermute | solution.py:301
  41.0 9.8 %collective-permute-start.14 = (bf16[128,1536]{1,0:T(8,128)(2,1)S(1)}, bf16[128,1536]{1,0:T(8,128)(2,1)S(1)}, u32[]{:S(2)}, u32[]{:S(2)}) collective-permute-start(bf16[128,1536]{1,0:T(8,128)(2,1)S(1)} %collective-permute-done.13.refs_14_.refs_6_), channel_id=1, source_target_pairs={{0,1},{1,0},{4,5},{5,4},{8,9},{9,8},{12,13},{13,12},{16,17},{17,16... | collective-permute-start | bytes 1179656 | tf_op jit(solution)/shard_map/ppermute | solution.py:301
  41.0 10.4 %collective-permute-start.12 = (bf16[128,1536]{1,0:T(8,128)(2,1)S(1)}, bf16[128,1536]{1,0:T(8,128)(2,1)S(1)}, u32[]{:S(2)}, u32[]{:S(2)}) collective-permute-start(bf16[128,1536]{1,0:T(8,128)(2,1)S(1)} %collective-permute-done.11.refs_12_.refs_4_), channel_id=1, source_target_pairs={{0,1},{1,0},{4,5},{5,4},{8,9},{9,8},{12,13},{13,12},{16,17},{17,16... | collective-permute-start | bytes 1179656 | tf_op jit(solution)/shard_map/ppermute | solution.py:301
  41.9 9.8 %collective-permute-start.10 = (bf16[128,1536]{1,0:T(8,128)(2,1)S(1)}, bf16[128,1536]{1,0:T(8,128)(2,1)S(1)}, u32[]{:S(2)}, u32[]{:S(2)}) collective-permute-start(bf16[128,1536]{1,0:T(8,128)(2,1)S(1)} %collective-permute-done.9.refs_10_.refs_2_), channel_id=1, source_target_pairs={{0,1},{1,0},{4,5},{5,4},{8,9},{9,8},{12,13},{13,12},{16,17},{17,16... | collective-permute-start | bytes 1179656 | tf_op jit(solution)/shard_map/ppermute | solution.py:301
  45.5 9.5 %collective-permute-start.1 = (bf16[128,1536]{1,0:T(8,128)(2,1)S(1)}, bf16[128,1536]{1,0:T(8,128)(2,1)S(1)}, u32[]{:S(2)}, u32[]{:S(2)}) collective-permute-start(bf16[128,1536]{1,0:T(8,128)(2,1)S(1)} %get-tuple-element.41.refs_0_), channel_id=1, source_target_pairs={{0,1},{1,0},{4,5},{5,4},{8,9},{9,8},{12,13},{13,12},{16,17},{17,16... | collective-permute-start | bytes 1179656 | tf_op jit(solution)/shard_map/ppermute | solution.py:301
  50.8 4.1 %collective-permute-start.7 = (bf16[128,1536]{1,0:T(8,128)(2,1)S(1)}, bf16[128,1536]{1,0:T(8,128)(2,1)S(1)}, u32[]{:S(2)}, u32[]{:S(2)}) collective-permute-start(bf16[128,1536]{1,0:T(8,128)(2,1)S(1)} %collective-permute-done.6.refs_6_), channel_id=1, source_target_pairs={{0,1},{1,0},{4,5},{5,4},{8,9},{9,8},{12,13},{13,12},{16,17},{17,16... | collective-permute-start | bytes 1179656 | tf_op jit(solution)/shard_map/ppermute | solution.py:301
  50.9 4.1 %collective-permute-start.5 = (bf16[128,1536]{1,0:T(8,128)(2,1)S(1)}, bf16[128,1536]{1,0:T(8,128)(2,1)S(1)}, u32[]{:S(2)}, u32[]{:S(2)}) collective-permute-start(bf16[128,1536]{1,0:T(8,128)(2,1)S(1)} %collective-permute-done.4.refs_4_), channel_id=1, source_target_pairs={{0,1},{1,0},{4,5},{5,4},{8,9},{9,8},{12,13},{13,12},{16,17},{17,16... | collective-permute-start | bytes 1179656 | tf_op jit(solution)/shard_map/ppermute | solution.py:301
  51.4 3.6 %collective-permute-start.3 = (bf16[128,1536]{1,0:T(8,128)(2,1)S(1)}, bf16[128,1536]{1,0:T(8,128)(2,1)S(1)}, u32[]{:S(2)}, u32[]{:S(2)}) collective-permute-start(bf16[128,1536]{1,0:T(8,128)(2,1)S(1)} %collective-permute-done.2.refs_2_), channel_id=1, source_target_pairs={{0,1},{1,0},{4,5},{5,4},{8,9},{9,8},{12,13},{13,12},{16,17},{17,16... | collective-permute-start | bytes 1179656 | tf_op jit(solution)/shard_map/ppermute | solution.py:301
  54.1 13.5 %collective-permute-start.18 = (bf16[128,1536]{1,0:T(8,128)(2,1)S(1)}, bf16[128,1536]{1,0:T(8,128)(2,1)S(1)}, u32[]{:S(2)}, u32[]{:S(2)}) collective-permute-start(bf16[128,1536]{1,0:T(8,128)(2,1)S(1)} %get-tuple-element.39), channel_id=1, source_target_pairs={{0,2},{1,3},{4,6},{5,7},{8,10},{9,11},{12,14},{13,15},{16,18},{17,... | collective-permute-start | bytes 1179656 | tf_op jit(solution)/shard_map/ppermute | solution.py:301
  59.0 20.6 %collective-permute-start.17 = (bf16[128,1536]{1,0:T(8,128)(2,1)}, bf16[128,1536]{1,0:T(8,128)(2,1)}, u32[]{:S(2)}, u32[]{:S(2)}) collective-permute-start(bf16[128,1536]{1,0:T(8,128)(2,1)} %get-tuple-element.37), channel_id=1, source_target_pairs={{0,2},{1,3},{4,6},{5,7},{8,10},{9,11},{12,14},{13,15},{16,18},{17,... | collective-permute-start | bytes 1179656 | tf_op jit(solution)/shard_map/ppermute | solution.py:301
  68.6 22.4 %all-to-all-start.2 = ((bf16[16,8,1536]{2,1,0:T(8,128)(2,1)}), bf16[16,8,1536]{2,1,0:T(8,128)(2,1)}, u32[]{:S(2)}, u32[]{:S(2)}) async-start(bf16[16,8,1536]{2,1,0:T(8,128)(2,1)} %fusion.1), calls=%async_computation.2 | async-start | bytes 786432 | tf_op jit(solution)/shard_map/all_to_all | solution.py:336
  77.3 35.8 %collective-permute-start = (bf16[128,3072]{1,0:T(8,128)(2,1)}, bf16[128,3072]{1,0:T(8,128)(2,1)}, u32[]{:S(2)}, u32[]{:S(2)}) collective-permute-start(bf16[128,3072]{1,0:T(8,128)(2,1)} %param.11), channel_id=1, source_target_pairs={{0,18},{1,19},{4,22},{5,23},{8,26},{9,27},{12,30},{13,31},{16,2},{... | collective-permute-start | bytes 2359304 | tf_op jit(solution)/shard_map/ppermute | solution.py:301
  90.9 16.3 %all-to-all-start = ((bf16[16,8,1536]{2,1,0:T(8,128)(2,1)}), bf16[16,8,1536]{2,1,0:T(8,128)(2,1)}, u32[]{:S(2)}, u32[]{:S(2)}) async-start(bf16[16,8,1536]{2,1,0:T(8,128)(2,1)} %fusion), calls=%async_computation | async-start | bytes 786432 | tf_op jit(solution)/shard_map/all_to_all | solution.py:336
  108.8 16.7 %all-to-all-start.3 = ((bf16[16,8,1536]{2,1,0:T(8,128)(2,1)}), bf16[16,8,1536]{2,1,0:T(8,128)(2,1)}, u32[]{:S(2)}, u32[]{:S(2)}) async-start(bf16[16,8,1536]{2,1,0:T(8,128)(2,1)} %broadcast_in_dim.21), calls=%async_computation.3 | async-start | bytes 786432 | tf_op jit(solution)/shard_map/all_to_all | solution.py:338
  122.7 20.9 %collective-permute-start.15 = (bf16[1024,128]{1,0:T(8,128)(2,1)}, bf16[1024,128]{1,0:T(8,128)(2,1)}, u32[]{:S(2)}, u32[]{:S(2)}) collective-permute-start(bf16[1024,128]{1,0:T(8,128)(2,1)} %get-tuple-element.23), channel_id=1, source_target_pairs={{0,2},{1,3},{4,6},{5,7},{8,10},{9,11},{12,14},{13,15},{16,18},{17,... | collective-permute-start | bytes 786440 | tf_op jit(solution)/shard_map/ppermute | solution.py:301
  126.3 23.5 %all-to-all-start.1 = ((bf16[16,8,1536]{2,1,0:T(8,128)(2,1)}), bf16[16,8,1536]{2,1,0:T(8,128)(2,1)S(1)}, u32[]{:S(2)}, u32[]{:S(2)}) async-start(bf16[16,8,1536]{2,1,0:T(8,128)(2,1)} %broadcast_in_dim.20), calls=%async_computation.1 | async-start | bytes 786432 | tf_op jit(solution)/shard_map/all_to_all | solution.py:338
  (41 other events, 206.6 us)

commit v2 on v0

v2 whole, which is shorter than its diff:
```python
import functools

import jax
import jax.numpy as jnp
from jax import lax
from jax.experimental import pallas as pl
from jax.experimental.pallas import tpu as pltpu
from jax.sharding import PartitionSpec as P

AXES = ("hst", "seq")
LOG2E = 1.4426950408889634
SUB = 256
FORWARD_SUB = 512
TOKENS = 128
VMEM = 58 << 20
FULL_Y = tuple(
    tuple((z * 2 + y_lo) * 16 + x * 4 + y_hi * 2 + core for y_hi in range(2) for z in range(8) for y_lo in range(2))
    for x in range(4)
    for core in range(2)
)


def pairs(move):
    out = []
    for z in range(8):
        for y in range(4):
            for x in range(4):
                for core in range(2):
                    nx, ny, nc = move(x, y, core)
                    nx, ny = nx % 4, ny % 4
                    here = (z * 2 + y % 2) * 16 + x * 4 + (y // 2) * 2 + core
                    there = (z * 2 + ny % 2) * 16 + nx * 4 + (ny // 2) * 2 + nc
                    out.append((here, there))
    return out


FROM_X1 = pairs(lambda x, y, core: (x - 1, y, core))
FROM_X3 = pairs(lambda x, y, core: (x + 1, y, core))
FROM_X2 = pairs(lambda x, y, core: (x + 2, y, core))
SWAP_CORE = pairs(lambda x, y, core: (x, y, 1 - core))
SWAP_Y = pairs(lambda x, y, core: (x, y + 2, core))
MIRROR_Y = pairs(lambda x, y, core: (x, 3 - y, core))


def send(array, perm):
    return lax.ppermute(array, AXES, perm)


def dot(left, right, left_dim, right_dim):
    return lax.dot_general(
        left, right, (((left_dim,), (right_dim,)), ((), ())), preferred_element_type=jnp.float32
    )


def shape(*dims, dtype=jnp.bfloat16):
    return jax.ShapeDtypeStruct(dims, dtype)


def call(kernel, name, cost, out_shape, scalars, operands, scratch=(), out_any=(), inner=False):
    smem = [pl.BlockSpec(memory_space=pltpu.SMEM)] * len(scalars)
    space = pltpu.VMEM if inner else pl.ANY
    out_specs = [
        pl.BlockSpec(memory_space=pl.ANY if index in out_any else pltpu.VMEM)
        for index in range(len(out_shape))
    ]
    return pl.pallas_call(
        kernel,
        in_specs=smem + [pl.BlockSpec(memory_space=space)] * len(operands),
        out_specs=out_specs,
        out_shape=out_shape,
        scratch_shapes=list(scratch),
        compiler_params=pltpu.CompilerParams(vmem_limit_bytes=(12 << 20) if inner else VMEM),
        cost_estimate=pl.CostEstimate(flops=cost, bytes_accessed=1 << 18, transcendentals=0),
        name=name,
    )(*scalars, *operands)


def vmem(*dims, dtype=jnp.bfloat16):
    return pltpu.VMEM(dims, dtype)


class Loads:
    def __init__(self, sems):
        self.sems, self.copies = sems, []

    def start(self, source, target):
        copy = pltpu.make_async_copy(source, target, self.sems.at[len(self.copies)])
        copy.start()
        self.copies.append(copy)
        return copy


def forward_kernel(scale, q_in, k_in, v_in, o_ref, inv_ref, p_out, q_ref, k_ref, v_ref, p_ref, load_sems, store_sems):
    loads = Loads(load_sems)
    rows, head_dim = q_ref.shape
    queries = loads.start(q_in, q_ref)
    keys = loads.start(k_in, k_ref)
    values = loads.start(v_in, v_ref)
    queries.wait()
    keys.wait()
    stores = []
    ones = jnp.ones(v_ref.shape, jnp.bfloat16)
    for index, start in enumerate(range(0, rows, FORWARD_SUB)):
        here = pl.ds(start, FORWARD_SUB)
        scores = dot(q_ref[here, :], k_ref[...], 1, 1)
        row_max = jnp.max(scores, axis=1, keepdims=True)
        weights = jnp.exp2((scores - row_max) * (scale * LOG2E)).astype(jnp.bfloat16)
        p_ref[here, :] = weights
        store = pltpu.make_async_copy(p_ref.at[here], p_out.at[here], store_sems.at[index])
        store.start()
        stores.append(store)
        if start == 0:
            values.wait()
        both = dot(weights, jnp.concatenate([v_ref[...], ones], axis=1), 1, 0)
        inverse = 1.0 / both[:, head_dim:]
        o_ref[here, :] = (both[:, :head_dim] * inverse).astype(jnp.bfloat16)
        inv_ref[here, :] = inverse
    for store in stores:
        store.wait()


def forward(queries, keys, values):
    rows, head_dim = queries.shape
    count = keys.shape[0]
    return call(
        functools.partial(forward_kernel, 1.0 / head_dim**0.5),
        "attention_forward",
        5 * 10**8,
        [shape(rows, head_dim), shape(rows, head_dim, dtype=jnp.float32), shape(rows, count)],
        (),
        (queries, keys, values),
        [
            vmem(rows, head_dim),
            vmem(count, head_dim),
            vmem(count, head_dim),
            vmem(rows, count),
            pltpu.SemaphoreType.DMA((3,)),
            pltpu.SemaphoreType.DMA((rows // FORWARD_SUB,)),
        ],
        out_any=(2,),
    )


def backward_kernel(scale, groups, at_ref, *refs):
    ins, (dq_ref, dk_ref, dv_ref), held, sems = refs[:10], refs[10:13], refs[13:21], refs[21]
    q_ref, k_ref, v_ref, o_ref, inv_ref, p_ref, ga_ref, gb_ref = held
    rows = q_ref.shape[0]
    loads = Loads(sems)
    first = [loads.start(ins[index], target) for index, target in ((2, v_ref), (3, o_ref), (4, inv_ref))]
    for source, target, flip in ((6, ga_ref, 0), (8, gb_ref, 1)):
        for index, keys in enumerate(groups):
            start = 0
            for key in keys:
                there = ins[source + index].at[pl.ds(start, key[-1])]
                first.append(loads.start(there, target.at[rows_of(at_ref, key, flip)]))
                start += key[-1]
    parts = [pl.ds(index * SUB, SUB) for index in range(rows // SUB)]
    weights = []

    def load_weights(part):
        weights.append(loads.start(ins[5].at[parts[part]], p_ref.at[parts[part]]))

    load_weights(0)
    first += [loads.start(ins[1], k_ref), loads.start(ins[0], q_ref)]
    for part in range(1, len(parts)):
        load_weights(part)
    for copy in first:
        copy.wait()
    dk = dv = None
    for here, arrived in zip(parts, weights):
        grad = ga_ref[here, :].astype(jnp.float32) + gb_ref[here, :].astype(jnp.float32)
        grad = grad * inv_ref[here, :]
        grad16 = grad.astype(jnp.bfloat16)
        delta = jnp.sum(grad * o_ref[here, :].astype(jnp.float32), axis=1, keepdims=True)
        grad_probs = dot(grad16, v_ref[...], 1, 1)
        arrived.wait()
        weights16 = p_ref[here, :]
        grad_scores = (weights16.astype(jnp.float32) * (grad_probs - delta)).astype(jnp.bfloat16)
        dq_ref[here, :] = (dot(grad_scores, k_ref[...], 1, 0) * scale).astype(jnp.bfloat16)
        dk_part = dot(q_ref[here, :], grad_scores, 0, 0)
        dv_part = dot(grad16, weights16, 0, 0)
        dk = dk_part if dk is None else dk + dk_part
        dv = dv_part if dv is None else dv + dv_part
    dk_ref[...] = (dk * scale).T.astype(jnp.bfloat16)
    dv_ref[...] = dv.T.astype(jnp.bfloat16)


def backward(at, groups, queries, keys, values, attn, inverse, weights, own, got):
    rows, head_dim = queries.shape
    out = shape(rows, head_dim)
    copies = 5 + 2 * sum(len(keys) for keys in groups) + rows // SUB
    return call(
        functools.partial(backward_kernel, 1.0 / head_dim**0.5, groups),
        "attention_backward",
        10**9,
        [out, out, out],
        (at,),
        (queries, keys, values, attn, inverse, weights, *own, *got),
        [
            vmem(rows, head_dim),
            vmem(rows, head_dim),
            vmem(rows, head_dim),
            vmem(rows, head_dim),
            vmem(rows, head_dim, dtype=jnp.float32),
            vmem(rows, keys.shape[0]),
            vmem(rows, head_dim),
            vmem(rows, head_dim),
            pltpu.SemaphoreType.DMA((copies,)),
        ],
    )


def rows_of(at_ref, block, flip=0):
    dx, e, y, start, size = block
    x = lax.rem(at_ref[0] + dx, 4)
    y_hi = at_ref[1] if y == flip else 1 - at_ref[1]
    core = at_ref[2] if e == 0 else 1 - at_ref[2]
    return pl.ds(pl.multiple_of((x * 4 + y_hi * 2 + core) * TOKENS + start, size), size)


def load_tokens(loads, blocks, tokens):
    columns = tokens.shape[1] // 2
    parts = []
    for part in range(2):
        here = pl.ds(part * columns, columns)
        copies, start = [], 0
        for block in blocks:
            size = block.shape[0]
            copies.append(loads.start(block.at[:, here], tokens.at[pl.ds(start, size), here]))
            start += size
        parts.append((here, copies))
    return parts


def projection_kernel(keys, at_ref, *refs):
    count = len(keys)
    ins, rest = refs[:2], refs[2:]
    blocks, rest = rest[:count], rest[count:]
    last = len(rest) == 7
    if last:
        gate_in, sum_in, out_ref, heads, tokens, (gate_ref, sum_ref), sems = rest
    else:
        out_ref, heads, tokens, sems = rest
    loads = Loads(sems)
    head_dim = ins[0].shape[1]
    small, start = [], 0
    for key in keys:
        here = pl.ds(start, key[-1])
        start += key[-1]
        for index, ref in enumerate(ins):
            target = heads.at[here, pl.ds(index * head_dim, head_dim)]
            small.append(loads.start(ref.at[rows_of(at_ref, key)], target))
    parts = load_tokens(loads, blocks, tokens)
    if last:
        columns = tokens.shape[1]
        begin = pl.multiple_of(at_ref[1] * columns, columns)
        small += [loads.start(gate_in.at[:, pl.ds(begin, columns)], gate_ref), loads.start(sum_in, sum_ref)]
    for copy in small:
        copy.wait()
    for part, (here, copies) in enumerate(parts):
        for copy in copies:
            copy.wait()
        grad = dot(heads[...], tokens[:, here], 0, 0)
        if not last:
            out_ref[:, here] = grad
            continue
        grad = ((grad + sum_ref[:, here]) * gate_ref[:, here]).astype(jnp.bfloat16)
        for head in range(2):
            for row in range(0, head_dim, 16):
                first = head * head_dim + row
                out_ref[row // 16 * 2 + part, pl.ds(head * 16, 16), :] = grad[first : first + 16]


def projection_grad(at, keys, attn_own, attn_other, blocks, *last):
    head_dim, columns = attn_own.shape[1], blocks[0].shape[1]
    count = sum(key[-1] for key in keys)
    scratch = [vmem(count, 2 * head_dim), vmem(count, columns)]
    out = shape(2 * head_dim, columns, dtype=jnp.float32)
    if last:
        out = shape(16, 32, columns // 2)
        scratch.append([vmem(1, columns, dtype=jnp.float32), vmem(2 * head_dim, columns, dtype=jnp.float32)])
    return call(
        functools.partial(projection_kernel, keys),
        "projection_grad",
        10**8,
        [out],
        (at,),
        (attn_own, attn_other, *blocks, *last),
        scratch + [pltpu.SemaphoreType.DMA((2 + 4 * len(keys),))],
    )[0]


def tokens_kernel(count, at_ref, own_in, other_in, gate_in, *refs):
    blocks, (own_out, other_out, own_w, other_w, gate_ref, tokens, sems) = refs[:count], refs[count:]
    loads = Loads(sems)
    head_dim, columns = own_w.shape
    mine = pl.ds(pl.multiple_of(at_ref[1] * columns, columns), columns)
    small = [
        loads.start(own_in.at[:, mine], own_w),
        loads.start(other_in, other_w),
        loads.start(gate_in.at[:, mine], gate_ref),
    ]
    parts = load_tokens(loads, blocks, tokens)
    for copy in small:
        copy.wait()
    total = None
    for here, copies in parts:
        weight = jnp.concatenate(
            [
                (ref[:, here].astype(jnp.float32) * gate_ref[:, here]).astype(jnp.bfloat16)
                for ref in (own_w, other_w)
            ],
            axis=0,
        )
        for copy in copies:
            copy.wait()
        part = dot(tokens[:, here], weight, 1, 1)
        total = part if total is None else total + part
    own_out[...] = total[:, :head_dim].astype(jnp.bfloat16)
    other_out[...] = total[:, head_dim:].astype(jnp.bfloat16)


def tokens_grad(at, own_w, other_w, gate, blocks):
    rows = sum(block.shape[0] for block in blocks)
    head_dim, columns = other_w.shape
    out = shape(rows, head_dim)
    return call(
        functools.partial(tokens_kernel, len(blocks)),
        "tokens_grad",
        10**8,
        [out, out],
        (at,),
        (own_w, other_w, gate, *blocks),
        [
            vmem(head_dim, columns),
            vmem(head_dim, columns),
            vmem(1, columns, dtype=jnp.float32),
            vmem(rows, columns),
            pltpu.SemaphoreType.DMA((3 + 2 * len(blocks),)),
        ],
    )


def sum_kernel(at_ref, pieces_ref, out_ref):
    count = pieces_ref.shape[0]
    total = pieces_ref[0].astype(jnp.float32)
    for index in range(1, count):
        total += pieces_ref[index].astype(jnp.float32)
    total = total.astype(jnp.bfloat16)
    y_hi = at_ref[1]
    for index in range(count):
        out_ref[y_hi * count + index] = total[:16]
        out_ref[(1 - y_hi) * count + index] = total[16:]


def sum_pieces(at, pieces):
    count, rows, columns = pieces.shape
    out = [shape(2 * count, rows // 2, columns)]
    return call(sum_kernel, "sum_pieces", 10**7, out, (at,), (pieces,), inner=True)[0]


def place_kernel(pieces_ref, out_ref):
    count, size, columns = pieces_ref.shape
    for index in range(count):
        half, piece = divmod(index, count // 2)
        rows = pl.ds(piece // 2 * size, size)
        here = pl.ds((half * 2 + piece % 2) * columns, columns)
        out_ref[rows, here] = pieces_ref[index].astype(jnp.float32)


def place_pieces(pieces):
    count, size, columns = pieces.shape
    out = [shape(count // 4 * size, 4 * columns, dtype=jnp.float32)]
    return call(place_kernel, "place_pieces", 10**7, out, (), (pieces,), inner=True)[0]


def after(array, *others):
    return lax.optimization_barrier((array, *others))[0]


def shards(queries, keys, values, cotangent, gate, w_out):
    query_head, key_head, value_head = queries[0, 0], keys[0, 0], values[0, 0]
    half = gate.shape[1] // 2
    seq = lax.axis_index("seq")
    y_hi = (seq // 2) % 2

    def columns(array, y):
        return lax.dynamic_slice_in_dim(array, y * half, half, 1)

    keep = columns(cotangent[0], y_hi)
    near, far, across = [send(keep, perm) for perm in (FROM_X1, FROM_X3, FROM_X2)]
    got = send(columns(cotangent[0], 1 - y_hi), SWAP_Y)
    w_other = send(columns(w_out, 1 - y_hi), MIRROR_Y)
    attn, inverse, weights = forward(query_head, key_head, value_head)
    at = jnp.stack([seq // 4, y_hi, seq % 2]).astype(jnp.int32)

    near, far, across, got, w_other, _ = lax.optimization_barrier((near, far, across, got, w_other, attn))
    early = [keep, near, across, far]
    swapped = [send(part, SWAP_CORE) for part in early]
    got, attn_on, swapped = lax.optimization_barrier((got, attn, swapped))
    then = [got] + [send(got, perm) for perm in (FROM_X1, FROM_X2, FROM_X3)]
    attn_other = send(attn_on, SWAP_Y)

    def ends(y):
        return [(dx, e, y, 0, TOKENS) for dx in range(4) for e in range(2)]

    early = [part for pair in zip(early, swapped) for part in pair]
    own_1, other_1 = tokens_grad(at, w_out, w_other, gate, early)
    theirs_1 = send(other_1, SWAP_Y)
    partial = projection_grad(at, ends(0), after(attn, own_1), attn_other, early)
    then = lax.optimization_barrier((*then, partial))[:4]
    then = [part for block in then for part in (block, send(block, SWAP_CORE))]
    pieces = projection_grad(at, ends(1), attn, attn_other, then, gate, partial)
    own_2, other_2 = tokens_grad(at, after(w_out, pieces), w_other, gate, then)
    theirs_2 = send(other_2, SWAP_Y)
    pieces = lax.all_to_all(after(pieces, theirs_1), "hst", 0, 0, tiled=True)
    summed = sum_pieces(at, after(pieces, theirs_2))
    dq, dk, dv = backward(
        at,
        (ends(0), ends(1)),
        query_head,
        key_head,
        value_head,
        attn,
        inverse,
        weights,
        (after(own_1, summed), own_2),
        (theirs_1, theirs_2),
    )
    everywhere = lax.all_to_all(summed, AXES, 0, 0, tiled=True, axis_index_groups=FULL_Y)
    grad_out_proj = place_pieces(everywhere)
    return dq[None, None], dk[None, None], dv[None, None], grad_out_proj


def solution(mesh):
    in_specs = (
        P("hst", "seq", None, None),
        P("hst", "seq", None, None),
        P("hst", "seq", None, None),
        P("hst", "seq", None),
        P("hst", None),
        P("seq", None),
    )
    out_specs = (
        P("hst", "seq", None, None),
        P("hst", "seq", None, None),
        P("hst", "seq", None, None),
        P("seq", None),
    )
    return jax.shard_map(shards, mesh=mesh, in_specs=in_specs, out_specs=out_specs, check_vma=False)
```

time: 471 us -> 131 us (0.28)
  waiting for transfers between devices: 354 us -> 43.3 us
  matrix products: 57.2 us -> 0 us
  Pallas kernels: 0 us -> 46.3 us
  starting transfers between devices: 5.94 us -> 36.3 us
  blocking collectives: 17.3 us -> 0 us
  between operations: 13.9 us -> 0.9 us
  other arithmetic: 8.64 us -> 0.59 us
  loops' own time: 5.63 us -> 0 us
    reduce_scatter x1 -> x0, waiting for transfers between devices: 129 us -> none  [shards(): lax.psum_scatter(contract_first(attn_tokens, proj_local).astype(jnp.bfloa...]
    psum x1 -> x0, waiting for transfers between devices: 127 us -> none  [shards(): grad_out_proj = lax.psum(host_grad, 'hst').astype(jnp.float32)]
    all_gather x1 -> x0, waiting for transfers between devices: 96.9 us -> none  [shards(): lax.all_gather(w_out, 'seq', axis=0, tiled=True)]
    dot_general x30 -> x0, matrix products: 57.2 us -> none  [the longest x13 28.4 us: contract_last(): lax.dot_general(left, right, (((1,), (1,)), ((), ())), preferred_element_...]
    pallas_call x0 -> x8, Pallas kernels: none -> 46.3 us  [call(): pl.pallas_call(kernel, in_specs=smem + [pl.BlockSpec(memory_space=space)]...]
    ppermute x0 -> x19, waiting for transfers between devices: none -> 28.2 us  [send(): return lax.ppermute(array, AXES, perm)]
    ppermute x0 -> x19, starting transfers between devices: none -> 20 us  [send(): return lax.ppermute(array, AXES, perm)]
    all_to_all x1 -> x0, blocking collectives: 17.3 us -> none  [shards(): lax.all_to_all(attn_head, 'seq', split_axis=0, concat_axis=1, tiled=True)]
  transfers between devices with their start and end apart: 4 -> 21, of which waited for: 3 -> 13; matrix products, arithmetic and copies ran while one was open for 3% -> 0% of each run, Pallas kernels for 0% -> 33%
where the time goes in v2:
time: 131 us
  Pallas kernels  46.3 us (35%)
  waiting for transfers between devices  43.3 us (33%)
  starting transfers between devices  36.3 us (28%)
  local copies, waits for them, and re-layouts  3.62 us (3%)
    pallas_call x8, Pallas kernels, call(): pl.pallas_call(kernel, in_specs=smem + [pl.BlockSpec(memory_space=space)]...  46.3 us
    ppermute x19, waiting for transfers between devices, send(): return lax.ppermute(array, AXES, perm)  28.2 us
    ppermute x19, starting transfers between devices, send(): return lax.ppermute(array, AXES, perm)  20 us
    all_to_all x1, waiting for transfers between devices, shards(): lax.all_to_all(summed, AXES, 0, 0, tiled=True, axis_index_groups=FULL_Y)  10.6 us
    all_to_all x1, starting transfers between devices, shards(): pieces = lax.all_to_all(after(pieces, theirs_1), 'hst', 0, 0, tiled=True)  9.37 us
    all_to_all x1, starting transfers between devices, shards(): lax.all_to_all(summed, AXES, 0, 0, tiled=True, axis_index_groups=FULL_Y)  6.94 us
    all_to_all x1, waiting for transfers between devices, shards(): pieces = lax.all_to_all(after(pieces, theirs_1), 'hst', 0, 0, tiled=True)  4.52 us
  transfers between devices with their start and end apart: 21, of which 13 were waited for; matrix products, arithmetic and copies ran while one was open for 0% of the time, Pallas kernels for 33%

profile of v2, /device:TPU:2, one launch (start us, length us, event | category | flops | bytes accessed | tf_op | source)
XLA Modules:
  0.0 131.0 jit_solution(11497591066940146762)
XLA Ops:
  0.7 1.2 dynamic-slice_bitcast_fusion
  1.9 2.3 %collective-permute-start = (bf16[128,1536]{1,0:T(8,128)(2,1)S(1)}, bf16[128,1536]{1,0:T(8,128)(2,1)S(1)}, u32[]{:S(2)}, u32[]{:S(2)}) collective-permute-start(bf16[128,1536]{1,0:T(8,128)(2,1)S(1)} %get-tuple-element.65.refs_0_.refs_2_), channel_id=1, source_target_pairs={{0,12},{1,13},{4,0},{5,1},{8,4},{9,5},{12,8},{13,9},{16,28},{17,29... | collective-permute-start | bytes 1179656 | tf_op jit(solution)/shard_map/ppermute | solution.py:46
  4.3 3.1 %collective-permute-start.2 = (bf16[128,1536]{1,0:T(8,128)(2,1)S(1)}, bf16[128,1536]{1,0:T(8,128)(2,1)S(1)}, u32[]{:S(2)}, u32[]{:S(2)}) collective-permute-start(bf16[128,1536]{1,0:T(8,128)(2,1)S(1)} %get-tuple-element.65.refs_0_.refs_2_), channel_id=1, source_target_pairs={{0,8},{1,9},{4,12},{5,13},{8,0},{9,1},{12,4},{13,5},{16,24},{17,25... | collective-permute-start | bytes 1179656 | tf_op jit(solution)/shard_map/ppermute | solution.py:46
  7.4 3.2 %collective-permute-start.3 = (bf16[128,1536]{1,0:T(8,128)(2,1)S(1)}, bf16[128,1536]{1,0:T(8,128)(2,1)S(1)}, u32[]{:S(2)}, u32[]{:S(2)}) collective-permute-start(bf16[128,1536]{1,0:T(8,128)(2,1)S(1)} %get-tuple-element.64), channel_id=1, source_target_pairs={{0,2},{1,3},{4,6},{5,7},{8,10},{9,11},{12,14},{13,15},{16,18},{17,... | collective-permute-start | bytes 1179656 | tf_op jit(solution)/shard_map/ppermute | solution.py:46
  11.7 10.0 %attention_forward.1 = (bf16[2048,128]{1,0:T(8,128)(2,1)}, f32[2048,128]{1,0:T(8,128)}, bf16[2048,2048]{1,0:T(8,128)(2,1)}) custom-call(bf16[2048,128]{1,0:T(8,128)(2,1)} %bitcast.13, bf16[2048,128]{1,0:T(8,128)(2,1)} %bitcast.15, bf16[2048,128]{1,0:T(8,128)(2,1)} %bitcast.17), custom_call_target="tpu_custom_call" | custom-call | flops 500000000 | bytes 262144 | tf_op jit(solution)/shard_map/attention_forward/pallas_call | solution.py:66
  22.2 5.1 %collective-permute-done.4.other_in = bf16[128,1536]{1,0:T(8,128)(2,1)S(1)} collective-permute-done((bf16[128,1536]{1,0:T(8,128)(2,1)S(1)}, bf16[128,1536]{1,0:T(8,128)(2,1)S(1)}, u32[]{:S(2)}, u32[]{:S(2)}) %collective-permute-start.4) | collective-permute-done | bytes 393248 | tf_op jit(solution)/shard_map/ppermute | solution.py:46
  27.9 1.2 collective-permute-done.6.refs_3_.refs_5_
  30.2 2.5 %collective-permute-start.9 = (bf16[2048,128]{1,0:T(8,128)(2,1)}, bf16[2048,128]{1,0:T(8,128)(2,1)S(1)}, u32[]{:S(2)}, u32[]{:S(2)}) collective-permute-start(bf16[2048,128]{1,0:T(8,128)(2,1)} %get-tuple-element.49.refs_0_.refs_3_), channel_id=1, source_target_pairs={{0,2},{1,3},{4,6},{5,7},{8,10},{9,11},{12,14},{13,15},{16,18},{17,... | collective-permute-start | bytes 1572872 | tf_op jit(solution)/shard_map/ppermute | solution.py:46
  33.9 1.9 %collective-permute-start.12 = (bf16[128,1536]{1,0:T(8,128)(2,1)S(1)}, bf16[128,1536]{1,0:T(8,128)(2,1)}, u32[]{:S(2)}, u32[]{:S(2)}) collective-permute-start(bf16[128,1536]{1,0:T(8,128)(2,1)S(1)} %collective-permute-done.3.refs_2_.refs_0_), channel_id=1, source_target_pairs={{0,4},{1,5},{4,8},{5,9},{8,12},{9,13},{12,0},{13,1},{16,20},{17,21... | collective-permute-start | bytes 1179656 | tf_op jit(solution)/shard_map/ppermute | solution.py:46
  36.3 4.7 %tokens_grad.2 = (bf16[1024,128]{1,0:T(8,128)(2,1)}, bf16[1024,128]{1,0:T(8,128)(2,1)}) custom-call(s32[3]{0:T(128)} %pad_add_fusion.at_ref, bf16[128,3072]{1,0:T(8,128)(2,1)} %own_in.2, bf16[128,1536]{1,0:T(8,128)(2,1)} %copy-done.18, f32[1,3072]{1,0:T(1,128)} %gate_in.3, bf16[128,1536]{1,0:T(8,128)(2,1)} %copy-done.2, bf16[128,1536]{1,0:T(8,128)(2,1)} %copy-done.10, ...), custom_call_target="tpu_custom_call" | custom-call | flops 100000000 | bytes 262144 | tf_op jit(solution)/shard_map/tokens_grad/pallas_call | solution.py:66
  41.0 4.8 %collective-permute-done.9.refs_1_ = bf16[2048,128]{1,0:T(8,128)(2,1)S(1)} collective-permute-done((bf16[2048,128]{1,0:T(8,128)(2,1)}, bf16[2048,128]{1,0:T(8,128)(2,1)S(1)}, u32[]{:S(2)}, u32[]{:S(2)}) %collective-permute-start.9) | collective-permute-done | bytes 524320 | tf_op jit(solution)/shard_map/ppermute | solution.py:46
  46.6 5.2 %projection_grad.2.refs_11_ = f32[256,1536]{1,0:T(8,128)} custom-call(s32[3]{0:T(128)} %pad_add_fusion.at_ref, bf16[2048,128]{1,0:T(8,128)(2,1)} %get-tuple-element.49.refs_0_.refs_3_, bf16[2048,128]{1,0:T(8,128)(2,1)} %copy-done.3, bf16[128,1536]{1,0:T(8,128)(2,1)} %copy-done.2, bf16[128,1536]{1,0:T(8,128)(2,1)} %copy-done.10, bf16[128,1536]{1,0:T(8,128)(2,1)} %copy-done.5, ...), custom_call_target="tpu_custom_call" | custom-call | flops 100000000 | bytes 262144 | tf_op jit(solution)/shard_map/projection_grad/pallas_call | solution.py:66
  52.0 1.9 %collective-permute-done.12.refs_8_.refs_6_ = bf16[128,1536]{1,0:T(8,128)(2,1)} collective-permute-done((bf16[128,1536]{1,0:T(8,128)(2,1)S(1)}, bf16[128,1536]{1,0:T(8,128)(2,1)}, u32[]{:S(2)}, u32[]{:S(2)}) %collective-permute-start.12) | collective-permute-done | bytes 393248 | tf_op jit(solution)/shard_map/ppermute | solution.py:46
  58.9 6.0 %projection_grad.3 = bf16[16,32,768]{2,1,0:T(8,128)(2,1)} custom-call(s32[3]{0:T(128)} %pad_add_fusion.at_ref, bf16[2048,128]{1,0:T(8,128)(2,1)} %get-tuple-element.49.refs_0_.refs_3_, bf16[2048,128]{1,0:T(8,128)(2,1)} %copy-done.3, bf16[128,1536]{1,0:T(8,128)(2,1)} %copy-done.4, bf16[128,1536]{1,0:T(8,128)(2,1)} %copy-done.14, bf16[128,1536]{1,0:T(8,128)(2,1)} %copy-done.8, ...), custom_call_target="tpu_custom_call" | custom-call | flops 100000000 | bytes 262144 | tf_op jit(solution)/shard_map/projection_grad/pallas_call | solution.py:66
  65.0 9.4 %all-to-all-start = ((bf16[16,32,768]{2,1,0:T(8,128)(2,1)}), bf16[16,32,768]{2,1,0:T(8,128)(2,1)S(1)}, u32[]{:S(2)}, u32[]{:S(2)}) async-start(bf16[16,32,768]{2,1,0:T(8,128)(2,1)} %projection_grad.3), calls=%async_computation | async-start | bytes 1572864 | tf_op jit(solution)/shard_map/all_to_all | solution.py:416
  74.3 4.8 %tokens_grad.3 = (bf16[1024,128]{1,0:T(8,128)(2,1)}, bf16[1024,128]{1,0:T(8,128)(2,1)}) custom-call(s32[3]{0:T(128)} %pad_add_fusion.at_ref, bf16[128,3072]{1,0:T(8,128)(2,1)} %own_in.2, bf16[128,1536]{1,0:T(8,128)(2,1)} %copy-done.18, f32[1,3072]{1,0:T(1,128)} %gate_in.3, bf16[128,1536]{1,0:T(8,128)(2,1)} %copy-done.4, bf16[128,1536]{1,0:T(8,128)(2,1)} %copy-done.14, ...), custom_call_target="tpu_custom_call" | custom-call | flops 100000000 | bytes 262144 | tf_op jit(solution)/shard_map/tokens_grad/pallas_call | solution.py:66
  79.1 2.1 %collective-permute-start.18 = (bf16[1024,128]{1,0:T(8,128)(2,1)}, bf16[1024,128]{1,0:T(8,128)(2,1)S(1)}, u32[]{:S(2)}, u32[]{:S(2)}) collective-permute-start(bf16[1024,128]{1,0:T(8,128)(2,1)} %get-tuple-element.57), channel_id=1, source_target_pairs={{0,2},{1,3},{4,6},{5,7},{8,10},{9,11},{12,14},{13,15},{16,18},{17,... | collective-permute-start | bytes 786440 | tf_op jit(solution)/shard_map/ppermute | solution.py:46
  81.2 12.2 %collective-permute-done.18.refs_9_ = bf16[1024,128]{1,0:T(8,128)(2,1)S(1)} collective-permute-done((bf16[1024,128]{1,0:T(8,128)(2,1)}, bf16[1024,128]{1,0:T(8,128)(2,1)S(1)}, u32[]{:S(2)}, u32[]{:S(2)}) %collective-permute-start.18) | collective-permute-done | bytes 262176 | tf_op jit(solution)/shard_map/ppermute | solution.py:46
  93.4 4.5 %all-to-all-done.pieces_ref = bf16[16,32,768]{2,1,0:T(8,128)(2,1)S(1)} async-done(((bf16[16,32,768]{2,1,0:T(8,128)(2,1)}), bf16[16,32,768]{2,1,0:T(8,128)(2,1)S(1)}, u32[]{:S(2)}, u32[]{:S(2)}) %all-to-all-start) | async-done | bytes 786464 | tf_op jit(solution)/shard_map/all_to_all | solution.py:416
  97.9 1.6 %sum_pieces.1 = bf16[32,16,768]{2,1,0:T(8,128)(2,1)} custom-call(s32[3]{0:T(128)S(1)} %copy-done, bf16[16,32,768]{2,1,0:T(8,128)(2,1)S(1)} %all-to-all-done.pieces_ref), custom_call_target="tpu_custom_call" | custom-call | flops 10000000 | bytes 262144 | tf_op jit(solution)/shard_map/sum_pieces/pallas_call | solution.py:66
  99.5 6.9 %all-to-all-start.1 = ((bf16[32,16,768]{2,1,0:T(8,128)(2,1)}), bf16[32,16,768]{2,1,0:T(8,128)(2,1)S(1)}, u32[]{:S(2)}, u32[]{:S(2)}) async-start(bf16[32,16,768]{2,1,0:T(8,128)(2,1)} %sum_pieces.1), calls=%async_computation.1 | async-start | bytes 1572864 | tf_op jit(solution)/shard_map/all_to_all | solution.py:430
  106.4 12.7 %attention_backward.1 = (bf16[2048,128]{1,0:T(8,128)(2,1)}, bf16[2048,128]{1,0:T(8,128)(2,1)}, bf16[2048,128]{1,0:T(8,128)(2,1)}) custom-call(s32[3]{0:T(128)} %pad_add_fusion.at_ref, bf16[2048,128]{1,0:T(8,128)(2,1)} %bitcast.14, bf16[2048,128]{1,0:T(8,128)(2,1)} %bitcast.16, bf16[2048,128]{1,0:T(8,128)(2,1)} %bitcast.18, ...), custom_call_target="tpu_custom_call" | custom-call | flops 1000000000 | bytes 262144 | tf_op jit(solution)/shard_map/attention_backward/pallas_call | solution.py:66
  119.1 10.6 %all-to-all-done.1.pieces_ref = bf16[32,16,768]{2,1,0:T(8,128)(2,1)S(1)} async-done(((bf16[32,16,768]{2,1,0:T(8,128)(2,1)}), bf16[32,16,768]{2,1,0:T(8,128)(2,1)S(1)}, u32[]{:S(2)}, u32[]{:S(2)}) %all-to-all-start.1) | async-done | bytes 786464 | tf_op jit(solution)/shard_map/all_to_all | solution.py:430
  129.7 1.2 place_pieces.1
  (73 shorter events, 10.8 us)
Async XLA Ops:
  1.9 34.4 %copy-start.2 = (bf16[128,1536]{1,0:T(8,128)(2,1)}, bf16[128,1536]{1,0:T(8,128)(2,1)S(1)}, u32[]{:S(2)}) copy-start(bf16[128,1536]{1,0:T(8,128)(2,1)S(1)} %get-tuple-element.65.refs_0_.refs_2_) | copy-start | bytes 1179652
  1.9 19.9 %collective-permute-start = (bf16[128,1536]{1,0:T(8,128)(2,1)S(1)}, bf16[128,1536]{1,0:T(8,128)(2,1)S(1)}, u32[]{:S(2)}, u32[]{:S(2)}) collective-permute-start(bf16[128,1536]{1,0:T(8,128)(2,1)S(1)} %get-tuple-element.65.refs_0_.refs_2_), channel_id=1, source_target_pairs={{0,12},{1,13},{4,0},{5,1},{8,4},{9,5},{12,8},{13,9},{16,28},{17,29... | collective-permute-start | bytes 1179656 | tf_op jit(solution)/shard_map/ppermute | solution.py:46
  4.3 17.6 %collective-permute-start.1 = (bf16[128,1536]{1,0:T(8,128)(2,1)S(1)}, bf16[128,1536]{1,0:T(8,128)(2,1)S(1)}, u32[]{:S(2)}, u32[]{:S(2)}) collective-permute-start(bf16[128,1536]{1,0:T(8,128)(2,1)S(1)} %get-tuple-element.65.refs_0_.refs_2_), channel_id=1, source_target_pairs={{0,4},{1,5},{4,8},{5,9},{8,12},{9,13},{12,0},{13,1},{16,20},{17,21... | collective-permute-start | bytes 1179656 | tf_op jit(solution)/shard_map/ppermute | solution.py:46
  4.3 17.9 %collective-permute-start.2 = (bf16[128,1536]{1,0:T(8,128)(2,1)S(1)}, bf16[128,1536]{1,0:T(8,128)(2,1)S(1)}, u32[]{:S(2)}, u32[]{:S(2)}) collective-permute-start(bf16[128,1536]{1,0:T(8,128)(2,1)S(1)} %get-tuple-element.65.refs_0_.refs_2_), channel_id=1, source_target_pairs={{0,8},{1,9},{4,12},{5,13},{8,0},{9,1},{12,4},{13,5},{16,24},{17,25... | collective-permute-start | bytes 1179656 | tf_op jit(solution)/shard_map/ppermute | solution.py:46
  7.4 14.9 %collective-permute-start.3 = (bf16[128,1536]{1,0:T(8,128)(2,1)S(1)}, bf16[128,1536]{1,0:T(8,128)(2,1)S(1)}, u32[]{:S(2)}, u32[]{:S(2)}) collective-permute-start(bf16[128,1536]{1,0:T(8,128)(2,1)S(1)} %get-tuple-element.64), channel_id=1, source_target_pairs={{0,2},{1,3},{4,6},{5,7},{8,10},{9,11},{12,14},{13,15},{16,18},{17,... | collective-permute-start | bytes 1179656 | tf_op jit(solution)/shard_map/ppermute | solution.py:46
  10.6 16.7 %collective-permute-start.4 = (bf16[128,1536]{1,0:T(8,128)(2,1)S(1)}, bf16[128,1536]{1,0:T(8,128)(2,1)S(1)}, u32[]{:S(2)}, u32[]{:S(2)}) collective-permute-start(bf16[128,1536]{1,0:T(8,128)(2,1)S(1)} %constant_dynamic-slice_fusion), channel_id=1, source_target_pairs={{0,18},{1,19},{4,22},{5,23},{8,26},{9,27},{12,30},{13,31},{16,2},{... | collective-permute-start | bytes 1179656 | tf_op jit(solution)/shard_map/ppermute | solution.py:46
  21.8 6.0 %collective-permute-start.5 = (bf16[128,1536]{1,0:T(8,128)(2,1)S(1)}, bf16[128,1536]{1,0:T(8,128)(2,1)S(1)}, u32[]{:S(2)}, u32[]{:S(2)}) collective-permute-start(bf16[128,1536]{1,0:T(8,128)(2,1)S(1)} %get-tuple-element.65.refs_0_.refs_2_), channel_id=1, source_target_pairs={{0,1},{1,0},{4,5},{5,4},{8,9},{9,8},{12,13},{13,12},{16,17},{17,16... | collective-permute-start | bytes 1179656 | tf_op jit(solution)/shard_map/ppermute | solution.py:46
  22.2 31.7 %copy-start.4 = (bf16[128,1536]{1,0:T(8,128)(2,1)}, bf16[128,1536]{1,0:T(8,128)(2,1)S(1)}, u32[]{:S(2)}) copy-start(bf16[128,1536]{1,0:T(8,128)(2,1)S(1)} %collective-permute-done.3.refs_2_.refs_0_) | copy-start | bytes 1179652
  27.3 1.7 %collective-permute-start.6 = (bf16[128,1536]{1,0:T(8,128)(2,1)S(1)}, bf16[128,1536]{1,0:T(8,128)(2,1)S(1)}, u32[]{:S(2)}, u32[]{:S(2)}) collective-permute-start(bf16[128,1536]{1,0:T(8,128)(2,1)S(1)} %collective-permute-done.refs_2_.refs_4_), channel_id=1, source_target_pairs={{0,1},{1,0},{4,5},{5,4},{8,9},{9,8},{12,13},{13,12},{16,17},{17,16... | collective-permute-start | bytes 1179656 | tf_op jit(solution)/shard_map/ppermute | solution.py:46
  27.3 2.3 %collective-permute-start.7 = (bf16[128,1536]{1,0:T(8,128)(2,1)S(1)}, bf16[128,1536]{1,0:T(8,128)(2,1)S(1)}, u32[]{:S(2)}, u32[]{:S(2)}) collective-permute-start(bf16[128,1536]{1,0:T(8,128)(2,1)S(1)} %collective-permute-done.2.refs_4_.refs_6_), channel_id=1, source_target_pairs={{0,1},{1,0},{4,5},{5,4},{8,9},{9,8},{12,13},{13,12},{16,17},{17,16... | collective-permute-start | bytes 1179656 | tf_op jit(solution)/shard_map/ppermute | solution.py:46
  27.8 2.3 %collective-permute-start.8 = (bf16[128,1536]{1,0:T(8,128)(2,1)S(1)}, bf16[128,1536]{1,0:T(8,128)(2,1)S(1)}, u32[]{:S(2)}, u32[]{:S(2)}) collective-permute-start(bf16[128,1536]{1,0:T(8,128)(2,1)S(1)} %collective-permute-done.1.refs_6_.refs_8_), channel_id=1, source_target_pairs={{0,1},{1,0},{4,5},{5,4},{8,9},{9,8},{12,13},{13,12},{16,17},{17,16... | collective-permute-start | bytes 1179656 | tf_op jit(solution)/shard_map/ppermute | solution.py:46
  30.2 15.7 %collective-permute-start.9 = (bf16[2048,128]{1,0:T(8,128)(2,1)}, bf16[2048,128]{1,0:T(8,128)(2,1)S(1)}, u32[]{:S(2)}, u32[]{:S(2)}) collective-permute-start(bf16[2048,128]{1,0:T(8,128)(2,1)} %get-tuple-element.49.refs_0_.refs_3_), channel_id=1, source_target_pairs={{0,2},{1,3},{4,6},{5,7},{8,10},{9,11},{12,14},{13,15},{16,18},{17,... | collective-permute-start | bytes 1572872 | tf_op jit(solution)/shard_map/ppermute | solution.py:46
  32.7 19.3 %collective-permute-start.10 = (bf16[128,1536]{1,0:T(8,128)(2,1)S(1)}, bf16[128,1536]{1,0:T(8,128)(2,1)S(1)}, u32[]{:S(2)}, u32[]{:S(2)}) collective-permute-start(bf16[128,1536]{1,0:T(8,128)(2,1)S(1)} %collective-permute-done.3.refs_2_.refs_0_), channel_id=1, source_target_pairs={{0,12},{1,13},{4,0},{5,1},{8,4},{9,5},{12,8},{13,9},{16,28},{17,29... | collective-permute-start | bytes 1179656 | tf_op jit(solution)/shard_map/ppermute | solution.py:46
  32.9 19.1 %collective-permute-start.11 = (bf16[128,1536]{1,0:T(8,128)(2,1)S(1)}, bf16[128,1536]{1,0:T(8,128)(2,1)S(1)}, u32[]{:S(2)}, u32[]{:S(2)}) collective-permute-start(bf16[128,1536]{1,0:T(8,128)(2,1)S(1)} %collective-permute-done.3.refs_2_.refs_0_), channel_id=1, source_target_pairs={{0,8},{1,9},{4,12},{5,13},{8,0},{9,1},{12,4},{13,5},{16,24},{17,25... | collective-permute-start | bytes 1179656 | tf_op jit(solution)/shard_map/ppermute | solution.py:46
  33.9 20.1 %collective-permute-start.12 = (bf16[128,1536]{1,0:T(8,128)(2,1)S(1)}, bf16[128,1536]{1,0:T(8,128)(2,1)}, u32[]{:S(2)}, u32[]{:S(2)}) collective-permute-start(bf16[128,1536]{1,0:T(8,128)(2,1)S(1)} %collective-permute-done.3.refs_2_.refs_0_), channel_id=1, source_target_pairs={{0,4},{1,5},{4,8},{5,9},{8,12},{9,13},{12,0},{13,1},{16,20},{17,21... | collective-permute-start | bytes 1179656 | tf_op jit(solution)/shard_map/ppermute | solution.py:46
  54.0 2.0 %collective-permute-start.13 = (bf16[128,1536]{1,0:T(8,128)(2,1)S(1)}, bf16[128,1536]{1,0:T(8,128)(2,1)S(1)}, u32[]{:S(2)}, u32[]{:S(2)}) collective-permute-start(bf16[128,1536]{1,0:T(8,128)(2,1)S(1)} %collective-permute-done.3.refs_2_.refs_0_), channel_id=1, source_target_pairs={{0,1},{1,0},{4,5},{5,4},{8,9},{9,8},{12,13},{13,12},{16,17},{17,16... | collective-permute-start | bytes 1179656 | tf_op jit(solution)/shard_map/ppermute | solution.py:46
  54.0 2.8 %collective-permute-start.14 = (bf16[128,1536]{1,0:T(8,128)(2,1)S(1)}, bf16[128,1536]{1,0:T(8,128)(2,1)S(1)}, u32[]{:S(2)}, u32[]{:S(2)}) collective-permute-start(bf16[128,1536]{1,0:T(8,128)(2,1)S(1)} %collective-permute-done.10.refs_4_.refs_2_), channel_id=1, source_target_pairs={{0,1},{1,0},{4,5},{5,4},{8,9},{9,8},{12,13},{13,12},{16,17},{17,16... | collective-permute-start | bytes 1179656 | tf_op jit(solution)/shard_map/ppermute | solution.py:46
  54.5 2.9 %collective-permute-start.15 = (bf16[128,1536]{1,0:T(8,128)(2,1)S(1)}, bf16[128,1536]{1,0:T(8,128)(2,1)S(1)}, u32[]{:S(2)}, u32[]{:S(2)}) collective-permute-start(bf16[128,1536]{1,0:T(8,128)(2,1)S(1)} %collective-permute-done.11.refs_6_.refs_4_), channel_id=1, source_target_pairs={{0,1},{1,0},{4,5},{5,4},{8,9},{9,8},{12,13},{13,12},{16,17},{17,16... | collective-permute-start | bytes 1179656 | tf_op jit(solution)/shard_map/ppermute | solution.py:46
  54.5 2.9 %collective-permute-start.16 = (bf16[128,1536]{1,0:T(8,128)(2,1)}, bf16[128,1536]{1,0:T(8,128)(2,1)S(1)}, u32[]{:S(2)}, u32[]{:S(2)}) collective-permute-start(bf16[128,1536]{1,0:T(8,128)(2,1)} %collective-permute-done.12.refs_8_.refs_6_), channel_id=1, source_target_pairs={{0,1},{1,0},{4,5},{5,4},{8,9},{9,8},{12,13},{13,12},{16,17},{17,16... | collective-permute-start | bytes 1179656 | tf_op jit(solution)/shard_map/ppermute | solution.py:46
  55.0 10.0 %collective-permute-start.17 = (bf16[1024,128]{1,0:T(8,128)(2,1)S(1)}, bf16[1024,128]{1,0:T(8,128)(2,1)S(1)}, u32[]{:S(2)}, u32[]{:S(2)}) collective-permute-start(bf16[1024,128]{1,0:T(8,128)(2,1)S(1)} %copy-done.21), channel_id=1, source_target_pairs={{0,2},{1,3},{4,6},{5,7},{8,10},{9,11},{12,14},{13,15},{16,18},{17,... | collective-permute-start | bytes 786440 | tf_op jit(solution)/shard_map/ppermute | solution.py:46
  65.0 32.9 %all-to-all-start = ((bf16[16,32,768]{2,1,0:T(8,128)(2,1)}), bf16[16,32,768]{2,1,0:T(8,128)(2,1)S(1)}, u32[]{:S(2)}, u32[]{:S(2)}) async-start(bf16[16,32,768]{2,1,0:T(8,128)(2,1)} %projection_grad.3), calls=%async_computation | async-start | bytes 1572864 | tf_op jit(solution)/shard_map/all_to_all | solution.py:416
  74.3 23.6 %copy-start = (s32[3]{0:T(128)S(1)}, s32[3]{0:T(128)}, u32[]{:S(2)}) copy-start(s32[3]{0:T(128)} %pad_add_fusion.at_ref) | copy-start | bytes 40
  79.1 14.3 %collective-permute-start.18 = (bf16[1024,128]{1,0:T(8,128)(2,1)}, bf16[1024,128]{1,0:T(8,128)(2,1)S(1)}, u32[]{:S(2)}, u32[]{:S(2)}) collective-permute-start(bf16[1024,128]{1,0:T(8,128)(2,1)} %get-tuple-element.57), channel_id=1, source_target_pairs={{0,2},{1,3},{4,6},{5,7},{8,10},{9,11},{12,14},{13,15},{16,18},{17,... | collective-permute-start | bytes 786440 | tf_op jit(solution)/shard_map/ppermute | solution.py:46
  99.5 30.3 %all-to-all-start.1 = ((bf16[32,16,768]{2,1,0:T(8,128)(2,1)}), bf16[32,16,768]{2,1,0:T(8,128)(2,1)S(1)}, u32[]{:S(2)}, u32[]{:S(2)}) async-start(bf16[32,16,768]{2,1,0:T(8,128)(2,1)} %sum_pieces.1), calls=%async_computation.1 | async-start | bytes 1572864 | tf_op jit(solution)/shard_map/all_to_all | solution.py:430
  (19 other events, 126.8 us)

commit v3 on v2

--- a/solution.py
+++ b/solution.py
@@ -56,7 +56,7 @@
     return jax.ShapeDtypeStruct(dims, dtype)
 
 
-def call(kernel, name, cost, out_shape, scalars, operands, scratch=(), out_any=(), inner=False):
+def call(kernel, name, cost, out_shape, scalars, operands, scratch=(), out_any=(), inner=False, limit=VMEM):
     smem = [pl.BlockSpec(memory_space=pltpu.SMEM)] * len(scalars)
     space = pltpu.VMEM if inner else pl.ANY
     out_specs = [
@@ -69,7 +69,7 @@
         out_specs=out_specs,
         out_shape=out_shape,
         scratch_shapes=list(scratch),
-        compiler_params=pltpu.CompilerParams(vmem_limit_bytes=(12 << 20) if inner else VMEM),
+        compiler_params=pltpu.CompilerParams(vmem_limit_bytes=(12 << 20) if inner else limit),
         cost_estimate=pl.CostEstimate(flops=cost, bytes_accessed=1 << 18, transcendentals=0),
         name=name,
     )(*scalars, *operands)
@@ -287,6 +287,7 @@
         (at,),
         (attn_own, attn_other, *blocks, *last),
         scratch + [pltpu.SemaphoreType.DMA((2 + 4 * len(keys),))],
+        limit=(20 << 20) if last else VMEM,
     )[0]
 
 
@@ -394,10 +395,9 @@
     attn, inverse, weights = forward(query_head, key_head, value_head)
     at = jnp.stack([seq // 4, y_hi, seq % 2]).astype(jnp.int32)
 
-    near, far, across, got, w_other, _ = lax.optimization_barrier((near, far, across, got, w_other, attn))
+    near, far, across, got, w_other, attn_on = lax.optimization_barrier((near, far, across, got, w_other, attn))
     early = [keep, near, across, far]
     swapped = [send(part, SWAP_CORE) for part in early]
-    got, attn_on, swapped = lax.optimization_barrier((got, attn, swapped))
     then = [got] + [send(got, perm) for perm in (FROM_X1, FROM_X2, FROM_X3)]
     attn_other = send(attn_on, SWAP_Y)
 

time: 131 us -> 128 us (0.977)
  waiting for transfers between devices: 43.3 us -> 38.9 us
  Pallas kernels: 46.3 us -> 44.2 us
  local copies, waits for them, and re-layouts: 3.62 us -> 5.38 us
    pallas_call x8, Pallas kernels: 46.3 us -> 44.2 us  [call(): pl.pallas_call(kernel, in_specs=smem + [pl.BlockSpec(memory_space=space)]...]
    ppermute x19, waiting for transfers between devices: 28.2 us -> 26.2 us  [send(): return lax.ppermute(array, AXES, perm)]
    unnamed x44 -> x50, local copies, waits for them, and re-layouts: 2.36 us -> 4.12 us
    all_to_all x1, waiting for transfers between devices: 4.52 us -> 3.14 us  [shards(): pieces = lax.all_to_all(after(pieces, theirs_1), 'hst', 0, 0, tiled=True)]
  transfers between devices with their start and end apart: 21 -> 21, of which waited for: 13 -> 12; matrix products, arithmetic and copies ran while one was open for 0% -> 1% of each run, Pallas kernels for 33% -> 33%
where the time goes in v3:
time: 128 us; the launch traced here: 127 us
  Pallas kernels  44.2 us (35%)
  waiting for transfers between devices  38.9 us (30%)
  starting transfers between devices  36.9 us (29%)
  local copies, waits for them, and re-layouts  5.38 us (4%)
    pallas_call x8, Pallas kernels, call(): pl.pallas_call(kernel, in_specs=smem + [pl.BlockSpec(memory_space=space)]...  44.2 us
    ppermute x19, waiting for transfers between devices, send(): return lax.ppermute(array, AXES, perm)  26.2 us
    ppermute x19, starting transfers between devices, send(): return lax.ppermute(array, AXES, perm)  19.9 us
    all_to_all x1, waiting for transfers between devices, shards(): lax.all_to_all(summed, AXES, 0, 0, tiled=True, axis_index_groups=FULL_Y)  9.64 us
    all_to_all x1, starting transfers between devices, shards(): pieces = lax.all_to_all(after(pieces, theirs_1), 'hst', 0, 0, tiled=True)  9.34 us
    all_to_all x1, starting transfers between devices, shards(): lax.all_to_all(summed, AXES, 0, 0, tiled=True, axis_index_groups=FULL_Y)  7.59 us
    unnamed x50, local copies, waits for them, and re-layouts  4.12 us
    all_to_all x1, waiting for transfers between devices, shards(): pieces = lax.all_to_all(after(pieces, theirs_1), 'hst', 0, 0, tiled=True)  3.14 us
  transfers between devices with their start and end apart: 21, of which 12 were waited for; matrix products, arithmetic and copies ran while one was open for 1% of the time, Pallas kernels for 33%

profile of v3, /device:TPU:2, one launch (start us, length us, event | category | flops | bytes accessed | tf_op | source)
XLA Modules:
  0.0 127.0 jit_solution(13767587624193280107)
XLA Ops:
  0.7 1.2 dynamic-slice_bitcast_fusion
  1.9 2.3 %collective-permute-start = (bf16[128,1536]{1,0:T(8,128)(2,1)S(1)}, bf16[128,1536]{1,0:T(8,128)(2,1)S(1)}, u32[]{:S(2)}, u32[]{:S(2)}) collective-permute-start(bf16[128,1536]{1,0:T(8,128)(2,1)S(1)} %get-tuple-element.55.refs_0_.refs_2_), channel_id=1, source_target_pairs={{0,12},{1,13},{4,0},{5,1},{8,4},{9,5},{12,8},{13,9},{16,28},{17,29... | collective-permute-start | bytes 1179656 | tf_op jit(solution)/shard_map/ppermute | solution.py:46
  4.3 3.1 %collective-permute-start.2 = (bf16[128,1536]{1,0:T(8,128)(2,1)S(1)}, bf16[128,1536]{1,0:T(8,128)(2,1)S(1)}, u32[]{:S(2)}, u32[]{:S(2)}) collective-permute-start(bf16[128,1536]{1,0:T(8,128)(2,1)S(1)} %get-tuple-element.55.refs_0_.refs_2_), channel_id=1, source_target_pairs={{0,8},{1,9},{4,12},{5,13},{8,0},{9,1},{12,4},{13,5},{16,24},{17,25... | collective-permute-start | bytes 1179656 | tf_op jit(solution)/shard_map/ppermute | solution.py:46
  7.4 3.2 %collective-permute-start.3 = (bf16[128,1536]{1,0:T(8,128)(2,1)S(1)}, bf16[128,1536]{1,0:T(8,128)(2,1)S(1)}, u32[]{:S(2)}, u32[]{:S(2)}) collective-permute-start(bf16[128,1536]{1,0:T(8,128)(2,1)S(1)} %get-tuple-element.54), channel_id=1, source_target_pairs={{0,2},{1,3},{4,6},{5,7},{8,10},{9,11},{12,14},{13,15},{16,18},{17,... | collective-permute-start | bytes 1179656 | tf_op jit(solution)/shard_map/ppermute | solution.py:46
  11.7 10.0 %attention_forward.1 = (bf16[2048,128]{1,0:T(8,128)(2,1)}, f32[2048,128]{1,0:T(8,128)}, bf16[2048,2048]{1,0:T(8,128)(2,1)}) custom-call(bf16[2048,128]{1,0:T(8,128)(2,1)} %bitcast.13, bf16[2048,128]{1,0:T(8,128)(2,1)} %bitcast.15, bf16[2048,128]{1,0:T(8,128)(2,1)} %bitcast.17), custom_call_target="tpu_custom_call" | custom-call | flops 500000000 | bytes 262144 | tf_op jit(solution)/shard_map/attention_forward/pallas_call | solution.py:66
  22.2 5.1 %collective-permute-done.4.other_in = bf16[128,1536]{1,0:T(8,128)(2,1)S(1)} collective-permute-done((bf16[128,1536]{1,0:T(8,128)(2,1)S(1)}, bf16[128,1536]{1,0:T(8,128)(2,1)S(1)}, u32[]{:S(2)}, u32[]{:S(2)}) %collective-permute-start.4) | collective-permute-done | bytes 393248 | tf_op jit(solution)/shard_map/ppermute | solution.py:46
  27.8 2.5 %collective-permute-start.9 = (bf16[2048,128]{1,0:T(8,128)(2,1)}, bf16[2048,128]{1,0:T(8,128)(2,1)S(1)}, u32[]{:S(2)}, u32[]{:S(2)}) collective-permute-start(bf16[2048,128]{1,0:T(8,128)(2,1)} %get-tuple-element.39.refs_0_.refs_3_), channel_id=1, source_target_pairs={{0,2},{1,3},{4,6},{5,7},{8,10},{9,11},{12,14},{13,15},{16,18},{17,... | collective-permute-start | bytes 1572872 | tf_op jit(solution)/shard_map/ppermute | solution.py:46
  32.5 1.8 %collective-permute-start.12 = (bf16[128,1536]{1,0:T(8,128)(2,1)S(1)}, bf16[128,1536]{1,0:T(8,128)(2,1)S(1)}, u32[]{:S(2)}, u32[]{:S(2)}) collective-permute-start(bf16[128,1536]{1,0:T(8,128)(2,1)S(1)} %collective-permute-done.3.refs_2_.refs_0_), channel_id=1, source_target_pairs={{0,4},{1,5},{4,8},{5,9},{8,12},{9,13},{12,0},{13,1},{16,20},{17,21... | collective-permute-start | bytes 1179656 | tf_op jit(solution)/shard_map/ppermute | solution.py:46
  35.0 4.7 %tokens_grad.2 = (bf16[1024,128]{1,0:T(8,128)(2,1)}, bf16[1024,128]{1,0:T(8,128)(2,1)}) custom-call(s32[3]{0:T(128)} %pad_add_fusion.at_ref, bf16[128,3072]{1,0:T(8,128)(2,1)} %own_in.2, bf16[128,1536]{1,0:T(8,128)(2,1)} %copy-done.22, f32[1,3072]{1,0:T(1,128)} %gate_in.3, bf16[128,1536]{1,0:T(8,128)(2,1)} %copy-done.16, bf16[128,1536]{1,0:T(8,128)(2,1)} %copy-done.19, ...), custom_call_target="tpu_custom_call" | custom-call | flops 100000000 | bytes 262144 | tf_op jit(solution)/shard_map/tokens_grad/pallas_call | solution.py:66
  39.7 3.7 %collective-permute-done.9.refs_1_ = bf16[2048,128]{1,0:T(8,128)(2,1)S(1)} collective-permute-done((bf16[2048,128]{1,0:T(8,128)(2,1)}, bf16[2048,128]{1,0:T(8,128)(2,1)S(1)}, u32[]{:S(2)}, u32[]{:S(2)}) %collective-permute-start.9) | collective-permute-done | bytes 524320 | tf_op jit(solution)/shard_map/ppermute | solution.py:46
  44.2 5.2 %projection_grad.2.refs_11_ = f32[256,1536]{1,0:T(8,128)} custom-call(s32[3]{0:T(128)} %pad_add_fusion.at_ref, bf16[2048,128]{1,0:T(8,128)(2,1)} %get-tuple-element.39.refs_0_.refs_3_, bf16[2048,128]{1,0:T(8,128)(2,1)} %copy-done.2, bf16[128,1536]{1,0:T(8,128)(2,1)} %copy-done.16, bf16[128,1536]{1,0:T(8,128)(2,1)} %copy-done.19, ...), custom_call_target="tpu_custom_call" | custom-call | flops 100000000 | bytes 262144 | tf_op jit(solution)/shard_map/projection_grad/pallas_call | solution.py:66
  50.4 1.9 %collective-permute-done.12.refs_8_.refs_6_ = bf16[128,1536]{1,0:T(8,128)(2,1)S(1)} collective-permute-done((bf16[128,1536]{1,0:T(8,128)(2,1)S(1)}, bf16[128,1536]{1,0:T(8,128)(2,1)S(1)}, u32[]{:S(2)}, u32[]{:S(2)}) %collective-permute-start.12) | collective-permute-done | bytes 393248 | tf_op jit(solution)/shard_map/ppermute | solution.py:46
  55.8 1.4 %copy-done = f32[256,1536]{1,0:T(8,128)S(1)} copy-done((f32[256,1536]{1,0:T(8,128)S(1)}, f32[256,1536]{1,0:T(8,128)}, u32[]{:S(2)}) %copy-start) | copy-done | bytes 1572888
  58.2 3.9 %projection_grad.3 = bf16[16,32,768]{2,1,0:T(8,128)(2,1)} custom-call(s32[3]{0:T(128)S(1)} %copy-done.13, bf16[2048,128]{1,0:T(8,128)(2,1)S(1)} %copy-done.1, bf16[2048,128]{1,0:T(8,128)(2,1)S(1)} %copy-done.3, bf16[128,1536]{1,0:T(8,128)(2,1)S(1)} %collective-permute-done.3.refs_2_.refs_0_, bf16[128,1536]{1,0:T(8,128)(2,1)S(1)} %collective-permute-done.13.refs_3_.refs_1_, ...), custom_call_target="tpu_custom_call" | custom-call | flops 100000000 | bytes 262144 | tf_op jit(solution)/shard_map/projection_grad/pallas_call | solution.py:66
  63.2 9.3 %all-to-all-start = ((bf16[16,32,768]{2,1,0:T(8,128)(2,1)}), bf16[16,32,768]{2,1,0:T(8,128)(2,1)S(1)}, u32[]{:S(2)}, u32[]{:S(2)}) async-start(bf16[16,32,768]{2,1,0:T(8,128)(2,1)} %projection_grad.3), calls=%async_computation | async-start | bytes 1572864 | tf_op jit(solution)/shard_map/all_to_all | solution.py:416
  72.5 4.8 %tokens_grad.3 = (bf16[1024,128]{1,0:T(8,128)(2,1)}, bf16[1024,128]{1,0:T(8,128)(2,1)}) custom-call(s32[3]{0:T(128)} %pad_add_fusion.at_ref, bf16[128,3072]{1,0:T(8,128)(2,1)} %own_in.2, bf16[128,1536]{1,0:T(8,128)(2,1)} %copy-done.22, f32[1,3072]{1,0:T(1,128)} %gate_in.3, bf16[128,1536]{1,0:T(8,128)(2,1)} %copy-done.4, bf16[128,1536]{1,0:T(8,128)(2,1)} %copy-done.8, ...), custom_call_target="tpu_custom_call" | custom-call | flops 100000000 | bytes 262144 | tf_op jit(solution)/shard_map/tokens_grad/pallas_call | solution.py:66
  77.4 1.9 %collective-permute-start.18 = (bf16[1024,128]{1,0:T(8,128)(2,1)}, bf16[1024,128]{1,0:T(8,128)(2,1)S(1)}, u32[]{:S(2)}, u32[]{:S(2)}) collective-permute-start(bf16[1024,128]{1,0:T(8,128)(2,1)} %get-tuple-element.47), channel_id=1, source_target_pairs={{0,2},{1,3},{4,6},{5,7},{8,10},{9,11},{12,14},{13,15},{16,18},{17,... | collective-permute-start | bytes 786440 | tf_op jit(solution)/shard_map/ppermute | solution.py:46
  79.3 11.8 %collective-permute-done.18.refs_9_ = bf16[1024,128]{1,0:T(8,128)(2,1)S(1)} collective-permute-done((bf16[1024,128]{1,0:T(8,128)(2,1)}, bf16[1024,128]{1,0:T(8,128)(2,1)S(1)}, u32[]{:S(2)}, u32[]{:S(2)}) %collective-permute-start.18) | collective-permute-done | bytes 262176 | tf_op jit(solution)/shard_map/ppermute | solution.py:46
  91.1 3.1 %all-to-all-done.pieces_ref = bf16[16,32,768]{2,1,0:T(8,128)(2,1)S(1)} async-done(((bf16[16,32,768]{2,1,0:T(8,128)(2,1)}), bf16[16,32,768]{2,1,0:T(8,128)(2,1)S(1)}, u32[]{:S(2)}, u32[]{:S(2)}) %all-to-all-start) | async-done | bytes 786464 | tf_op jit(solution)/shard_map/all_to_all | solution.py:416
  94.2 1.6 %sum_pieces.1 = bf16[32,16,768]{2,1,0:T(8,128)(2,1)} custom-call(s32[3]{0:T(128)S(1)} %copy-done.14, bf16[16,32,768]{2,1,0:T(8,128)(2,1)S(1)} %all-to-all-done.pieces_ref), custom_call_target="tpu_custom_call" | custom-call | flops 10000000 | bytes 262144 | tf_op jit(solution)/shard_map/sum_pieces/pallas_call | solution.py:66
  95.8 7.6 %all-to-all-start.1 = ((bf16[32,16,768]{2,1,0:T(8,128)(2,1)}), bf16[32,16,768]{2,1,0:T(8,128)(2,1)S(1)}, u32[]{:S(2)}, u32[]{:S(2)}) async-start(bf16[32,16,768]{2,1,0:T(8,128)(2,1)} %sum_pieces.1), calls=%async_computation.1 | async-start | bytes 1572864 | tf_op jit(solution)/shard_map/all_to_all | solution.py:430
  103.4 12.7 %attention_backward.1 = (bf16[2048,128]{1,0:T(8,128)(2,1)}, bf16[2048,128]{1,0:T(8,128)(2,1)}, bf16[2048,128]{1,0:T(8,128)(2,1)}) custom-call(s32[3]{0:T(128)} %pad_add_fusion.at_ref, bf16[2048,128]{1,0:T(8,128)(2,1)} %bitcast.14, bf16[2048,128]{1,0:T(8,128)(2,1)} %bitcast.16, bf16[2048,128]{1,0:T(8,128)(2,1)} %bitcast.18, ...), custom_call_target="tpu_custom_call" | custom-call | flops 1000000000 | bytes 262144 | tf_op jit(solution)/shard_map/attention_backward/pallas_call | solution.py:66
  116.1 9.6 %all-to-all-done.1.pieces_ref = bf16[32,16,768]{2,1,0:T(8,128)(2,1)S(1)} async-done(((bf16[32,16,768]{2,1,0:T(8,128)(2,1)}), bf16[32,16,768]{2,1,0:T(8,128)(2,1)S(1)}, u32[]{:S(2)}, u32[]{:S(2)}) %all-to-all-start.1) | async-done | bytes 786464 | tf_op jit(solution)/shard_map/all_to_all | solution.py:430
  125.7 1.2 place_pieces.1
  (79 shorter events, 12.2 us)
Async XLA Ops:
  1.9 33.0 %copy-start.16 = (bf16[128,1536]{1,0:T(8,128)(2,1)}, bf16[128,1536]{1,0:T(8,128)(2,1)S(1)}, u32[]{:S(2)}) copy-start(bf16[128,1536]{1,0:T(8,128)(2,1)S(1)} %get-tuple-element.55.refs_0_.refs_2_) | copy-start | bytes 1179652
  1.9 19.9 %collective-permute-start = (bf16[128,1536]{1,0:T(8,128)(2,1)S(1)}, bf16[128,1536]{1,0:T(8,128)(2,1)S(1)}, u32[]{:S(2)}, u32[]{:S(2)}) collective-permute-start(bf16[128,1536]{1,0:T(8,128)(2,1)S(1)} %get-tuple-element.55.refs_0_.refs_2_), channel_id=1, source_target_pairs={{0,12},{1,13},{4,0},{5,1},{8,4},{9,5},{12,8},{13,9},{16,28},{17,29... | collective-permute-start | bytes 1179656 | tf_op jit(solution)/shard_map/ppermute | solution.py:46
  4.3 17.6 %collective-permute-start.1 = (bf16[128,1536]{1,0:T(8,128)(2,1)S(1)}, bf16[128,1536]{1,0:T(8,128)(2,1)}, u32[]{:S(2)}, u32[]{:S(2)}) collective-permute-start(bf16[128,1536]{1,0:T(8,128)(2,1)S(1)} %get-tuple-element.55.refs_0_.refs_2_), channel_id=1, source_target_pairs={{0,4},{1,5},{4,8},{5,9},{8,12},{9,13},{12,0},{13,1},{16,20},{17,21... | collective-permute-start | bytes 1179656 | tf_op jit(solution)/shard_map/ppermute | solution.py:46
  4.3 17.9 %collective-permute-start.2 = (bf16[128,1536]{1,0:T(8,128)(2,1)S(1)}, bf16[128,1536]{1,0:T(8,128)(2,1)S(1)}, u32[]{:S(2)}, u32[]{:S(2)}) collective-permute-start(bf16[128,1536]{1,0:T(8,128)(2,1)S(1)} %get-tuple-element.55.refs_0_.refs_2_), channel_id=1, source_target_pairs={{0,8},{1,9},{4,12},{5,13},{8,0},{9,1},{12,4},{13,5},{16,24},{17,25... | collective-permute-start | bytes 1179656 | tf_op jit(solution)/shard_map/ppermute | solution.py:46
  7.4 14.9 %collective-permute-start.3 = (bf16[128,1536]{1,0:T(8,128)(2,1)S(1)}, bf16[128,1536]{1,0:T(8,128)(2,1)S(1)}, u32[]{:S(2)}, u32[]{:S(2)}) collective-permute-start(bf16[128,1536]{1,0:T(8,128)(2,1)S(1)} %get-tuple-element.54), channel_id=1, source_target_pairs={{0,2},{1,3},{4,6},{5,7},{8,10},{9,11},{12,14},{13,15},{16,18},{17,... | collective-permute-start | bytes 1179656 | tf_op jit(solution)/shard_map/ppermute | solution.py:46
  10.6 16.7 %collective-permute-start.4 = (bf16[128,1536]{1,0:T(8,128)(2,1)S(1)}, bf16[128,1536]{1,0:T(8,128)(2,1)S(1)}, u32[]{:S(2)}, u32[]{:S(2)}) collective-permute-start(bf16[128,1536]{1,0:T(8,128)(2,1)S(1)} %constant_dynamic-slice_fusion), channel_id=1, source_target_pairs={{0,18},{1,19},{4,22},{5,23},{8,26},{9,27},{12,30},{13,31},{16,2},{... | collective-permute-start | bytes 1179656 | tf_op jit(solution)/shard_map/ppermute | solution.py:46
  21.8 8.6 %collective-permute-start.5 = (bf16[128,1536]{1,0:T(8,128)(2,1)S(1)}, bf16[128,1536]{1,0:T(8,128)(2,1)S(1)}, u32[]{:S(2)}, u32[]{:S(2)}) collective-permute-start(bf16[128,1536]{1,0:T(8,128)(2,1)S(1)} %get-tuple-element.55.refs_0_.refs_2_), channel_id=1, source_target_pairs={{0,1},{1,0},{4,5},{5,4},{8,9},{9,8},{12,13},{13,12},{16,17},{17,16... | collective-permute-start | bytes 1179656 | tf_op jit(solution)/shard_map/ppermute | solution.py:46
  22.2 33.5 %copy-start.4 = (bf16[128,1536]{1,0:T(8,128)(2,1)}, bf16[128,1536]{1,0:T(8,128)(2,1)S(1)}, u32[]{:S(2)}) copy-start(bf16[128,1536]{1,0:T(8,128)(2,1)S(1)} %collective-permute-done.3.refs_2_.refs_0_) | copy-start | bytes 1179652
  27.3 3.4 %collective-permute-start.6 = (bf16[128,1536]{1,0:T(8,128)(2,1)S(1)}, bf16[128,1536]{1,0:T(8,128)(2,1)S(1)}, u32[]{:S(2)}, u32[]{:S(2)}) collective-permute-start(bf16[128,1536]{1,0:T(8,128)(2,1)S(1)} %collective-permute-done.refs_2_.refs_4_), channel_id=1, source_target_pairs={{0,1},{1,0},{4,5},{5,4},{8,9},{9,8},{12,13},{13,12},{16,17},{17,16... | collective-permute-start | bytes 1179656 | tf_op jit(solution)/shard_map/ppermute | solution.py:46
  27.3 4.4 %collective-permute-start.7 = (bf16[128,1536]{1,0:T(8,128)(2,1)S(1)}, bf16[128,1536]{1,0:T(8,128)(2,1)S(1)}, u32[]{:S(2)}, u32[]{:S(2)}) collective-permute-start(bf16[128,1536]{1,0:T(8,128)(2,1)S(1)} %collective-permute-done.2.refs_4_.refs_6_), channel_id=1, source_target_pairs={{0,1},{1,0},{4,5},{5,4},{8,9},{9,8},{12,13},{13,12},{16,17},{17,16... | collective-permute-start | bytes 1179656 | tf_op jit(solution)/shard_map/ppermute | solution.py:46
  27.8 15.6 %collective-permute-start.9 = (bf16[2048,128]{1,0:T(8,128)(2,1)}, bf16[2048,128]{1,0:T(8,128)(2,1)S(1)}, u32[]{:S(2)}, u32[]{:S(2)}) collective-permute-start(bf16[2048,128]{1,0:T(8,128)(2,1)} %get-tuple-element.39.refs_0_.refs_3_), channel_id=1, source_target_pairs={{0,2},{1,3},{4,6},{5,7},{8,10},{9,11},{12,14},{13,15},{16,18},{17,... | collective-permute-start | bytes 1572872 | tf_op jit(solution)/shard_map/ppermute | solution.py:46
  30.4 4.6 %collective-permute-start.8 = (bf16[128,1536]{1,0:T(8,128)(2,1)}, bf16[128,1536]{1,0:T(8,128)(2,1)}, u32[]{:S(2)}, u32[]{:S(2)}) collective-permute-start(bf16[128,1536]{1,0:T(8,128)(2,1)} %collective-permute-done.1.refs_6_.refs_8_), channel_id=1, source_target_pairs={{0,1},{1,0},{4,5},{5,4},{8,9},{9,8},{12,13},{13,12},{16,17},{17,16... | collective-permute-start | bytes 1179656 | tf_op jit(solution)/shard_map/ppermute | solution.py:46
  30.4 20.0 %collective-permute-start.10 = (bf16[128,1536]{1,0:T(8,128)(2,1)S(1)}, bf16[128,1536]{1,0:T(8,128)(2,1)S(1)}, u32[]{:S(2)}, u32[]{:S(2)}) collective-permute-start(bf16[128,1536]{1,0:T(8,128)(2,1)S(1)} %collective-permute-done.3.refs_2_.refs_0_), channel_id=1, source_target_pairs={{0,12},{1,13},{4,0},{5,1},{8,4},{9,5},{12,8},{13,9},{16,28},{17,29... | collective-permute-start | bytes 1179656 | tf_op jit(solution)/shard_map/ppermute | solution.py:46
  30.7 19.7 %collective-permute-start.11 = (bf16[128,1536]{1,0:T(8,128)(2,1)S(1)}, bf16[128,1536]{1,0:T(8,128)(2,1)S(1)}, u32[]{:S(2)}, u32[]{:S(2)}) collective-permute-start(bf16[128,1536]{1,0:T(8,128)(2,1)S(1)} %collective-permute-done.3.refs_2_.refs_0_), channel_id=1, source_target_pairs={{0,8},{1,9},{4,12},{5,13},{8,0},{9,1},{12,4},{13,5},{16,24},{17,25... | collective-permute-start | bytes 1179656 | tf_op jit(solution)/shard_map/ppermute | solution.py:46
  32.5 19.8 %collective-permute-start.12 = (bf16[128,1536]{1,0:T(8,128)(2,1)S(1)}, bf16[128,1536]{1,0:T(8,128)(2,1)S(1)}, u32[]{:S(2)}, u32[]{:S(2)}) collective-permute-start(bf16[128,1536]{1,0:T(8,128)(2,1)S(1)} %collective-permute-done.3.refs_2_.refs_0_), channel_id=1, source_target_pairs={{0,4},{1,5},{4,8},{5,9},{8,12},{9,13},{12,0},{13,1},{16,20},{17,21... | collective-permute-start | bytes 1179656 | tf_op jit(solution)/shard_map/ppermute | solution.py:46
  52.3 2.0 %collective-permute-start.13 = (bf16[128,1536]{1,0:T(8,128)(2,1)S(1)}, bf16[128,1536]{1,0:T(8,128)(2,1)S(1)}, u32[]{:S(2)}, u32[]{:S(2)}) collective-permute-start(bf16[128,1536]{1,0:T(8,128)(2,1)S(1)} %collective-permute-done.3.refs_2_.refs_0_), channel_id=1, source_target_pairs={{0,1},{1,0},{4,5},{5,4},{8,9},{9,8},{12,13},{13,12},{16,17},{17,16... | collective-permute-start | bytes 1179656 | tf_op jit(solution)/shard_map/ppermute | solution.py:46
  52.3 2.3 %collective-permute-start.14 = (bf16[128,1536]{1,0:T(8,128)(2,1)S(1)}, bf16[128,1536]{1,0:T(8,128)(2,1)S(1)}, u32[]{:S(2)}, u32[]{:S(2)}) collective-permute-start(bf16[128,1536]{1,0:T(8,128)(2,1)S(1)} %collective-permute-done.10.refs_4_.refs_2_), channel_id=1, source_target_pairs={{0,1},{1,0},{4,5},{5,4},{8,9},{9,8},{12,13},{13,12},{16,17},{17,16... | collective-permute-start | bytes 1179656 | tf_op jit(solution)/shard_map/ppermute | solution.py:46
  52.8 2.3 %collective-permute-start.15 = (bf16[128,1536]{1,0:T(8,128)(2,1)S(1)}, bf16[128,1536]{1,0:T(8,128)(2,1)S(1)}, u32[]{:S(2)}, u32[]{:S(2)}) collective-permute-start(bf16[128,1536]{1,0:T(8,128)(2,1)S(1)} %collective-permute-done.11.refs_6_.refs_4_), channel_id=1, source_target_pairs={{0,1},{1,0},{4,5},{5,4},{8,9},{9,8},{12,13},{13,12},{16,17},{17,16... | collective-permute-start | bytes 1179656 | tf_op jit(solution)/shard_map/ppermute | solution.py:46
  52.8 2.9 %collective-permute-start.16 = (bf16[128,1536]{1,0:T(8,128)(2,1)S(1)}, bf16[128,1536]{1,0:T(8,128)(2,1)S(1)}, u32[]{:S(2)}, u32[]{:S(2)}) collective-permute-start(bf16[128,1536]{1,0:T(8,128)(2,1)S(1)} %collective-permute-done.12.refs_8_.refs_6_), channel_id=1, source_target_pairs={{0,1},{1,0},{4,5},{5,4},{8,9},{9,8},{12,13},{13,12},{16,17},{17,16... | collective-permute-start | bytes 1179656 | tf_op jit(solution)/shard_map/ppermute | solution.py:46
  53.4 9.8 %collective-permute-start.17 = (bf16[1024,128]{1,0:T(8,128)(2,1)S(1)}, bf16[1024,128]{1,0:T(8,128)(2,1)}, u32[]{:S(2)}, u32[]{:S(2)}) collective-permute-start(bf16[1024,128]{1,0:T(8,128)(2,1)S(1)} %copy-done.24), channel_id=1, source_target_pairs={{0,2},{1,3},{4,6},{5,7},{8,10},{9,11},{12,14},{13,15},{16,18},{17,... | collective-permute-start | bytes 786440 | tf_op jit(solution)/shard_map/ppermute | solution.py:46
  63.2 31.0 %all-to-all-start = ((bf16[16,32,768]{2,1,0:T(8,128)(2,1)}), bf16[16,32,768]{2,1,0:T(8,128)(2,1)S(1)}, u32[]{:S(2)}, u32[]{:S(2)}) async-start(bf16[16,32,768]{2,1,0:T(8,128)(2,1)} %projection_grad.3), calls=%async_computation | async-start | bytes 1572864 | tf_op jit(solution)/shard_map/all_to_all | solution.py:416
  72.5 21.7 %copy-start.14 = (s32[3]{0:T(128)S(1)}, s32[3]{0:T(128)}, u32[]{:S(2)}) copy-start(s32[3]{0:T(128)} %pad_add_fusion.at_ref) | copy-start | bytes 40
  77.4 13.7 %collective-permute-start.18 = (bf16[1024,128]{1,0:T(8,128)(2,1)}, bf16[1024,128]{1,0:T(8,128)(2,1)S(1)}, u32[]{:S(2)}, u32[]{:S(2)}) collective-permute-start(bf16[1024,128]{1,0:T(8,128)(2,1)} %get-tuple-element.47), channel_id=1, source_target_pairs={{0,2},{1,3},{4,6},{5,7},{8,10},{9,11},{12,14},{13,15},{16,18},{17,... | collective-permute-start | bytes 786440 | tf_op jit(solution)/shard_map/ppermute | solution.py:46
  95.8 29.9 %all-to-all-start.1 = ((bf16[32,16,768]{2,1,0:T(8,128)(2,1)}), bf16[32,16,768]{2,1,0:T(8,128)(2,1)S(1)}, u32[]{:S(2)}, u32[]{:S(2)}) async-start(bf16[32,16,768]{2,1,0:T(8,128)(2,1)} %sum_pieces.1), calls=%async_computation.1 | async-start | bytes 1572864 | tf_op jit(solution)/shard_map/all_to_all | solution.py:430
  (22 other events, 170.2 us)

commit v4 on v3

--- a/solution.py
+++ b/solution.py
@@ -408,12 +408,12 @@
     own_1, other_1 = tokens_grad(at, w_out, w_other, gate, early)
     theirs_1 = send(other_1, SWAP_Y)
     partial = projection_grad(at, ends(0), after(attn, own_1), attn_other, early)
-    then = lax.optimization_barrier((*then, partial))[:4]
+    then = lax.optimization_barrier((*then, partial, theirs_1))[:4]
     then = [part for block in then for part in (block, send(block, SWAP_CORE))]
     pieces = projection_grad(at, ends(1), attn, attn_other, then, gate, partial)
     own_2, other_2 = tokens_grad(at, after(w_out, pieces), w_other, gate, then)
     theirs_2 = send(other_2, SWAP_Y)
-    pieces = lax.all_to_all(after(pieces, theirs_1), "hst", 0, 0, tiled=True)
+    pieces = lax.all_to_all(pieces, "hst", 0, 0, tiled=True)
     summed = sum_pieces(at, after(pieces, theirs_2))
     dq, dk, dv = backward(
         at,

time: 128 us -> 130 us (1.016)
  waiting for transfers between devices: 38.9 us -> 40.6 us
  local copies, waits for them, and re-layouts: 5.38 us -> 6.86 us
    unnamed x50 -> x48, local copies, waits for them, and re-layouts: 4.12 us -> 5.6 us
    all_to_all x1, waiting for transfers between devices: 3.14 us -> 4.45 us  [shards(): pieces = lax.all_to_all(pieces, 'hst', 0, 0, tiled=True)]
  transfers between devices with their start and end apart: 21 -> 21, of which waited for: 12 -> 11; matrix products, arithmetic and copies ran while one was open for 1% -> 1% of each run, Pallas kernels for 33% -> 29%
where the time goes in v4:
time: 130 us
  Pallas kernels  44.1 us (34%)
  waiting for transfers between devices  40.6 us (31%)
  starting transfers between devices  36.3 us (28%)
  local copies, waits for them, and re-layouts  6.86 us (5%)
    pallas_call x8, Pallas kernels, call(): pl.pallas_call(kernel, in_specs=smem + [pl.BlockSpec(memory_space=space)]...  44.1 us
    ppermute x19, waiting for transfers between devices, send(): return lax.ppermute(array, AXES, perm)  25.4 us
    ppermute x19, starting transfers between devices, send(): return lax.ppermute(array, AXES, perm)  20 us
    all_to_all x1, waiting for transfers between devices, shards(): lax.all_to_all(summed, AXES, 0, 0, tiled=True, axis_index_groups=FULL_Y)  10.8 us
    all_to_all x1, starting transfers between devices, shards(): pieces = lax.all_to_all(pieces, 'hst', 0, 0, tiled=True)  9.35 us
    all_to_all x1, starting transfers between devices, shards(): lax.all_to_all(summed, AXES, 0, 0, tiled=True, axis_index_groups=FULL_Y)  6.97 us
    unnamed x48, local copies, waits for them, and re-layouts  5.6 us
    all_to_all x1, waiting for transfers between devices, shards(): pieces = lax.all_to_all(pieces, 'hst', 0, 0, tiled=True)  4.45 us
  transfers between devices with their start and end apart: 21, of which 11 were waited for; matrix products, arithmetic and copies ran while one was open for 1% of the time, Pallas kernels for 29%

profile of v4, /device:TPU:2, one launch (start us, length us, event | category | flops | bytes accessed | tf_op | source)
XLA Modules:
  0.0 129.6 jit_solution(633995213609285304)
XLA Ops:
  0.7 1.2 dynamic-slice_bitcast_fusion
  1.9 2.3 %collective-permute-start = (bf16[128,1536]{1,0:T(8,128)(2,1)S(1)}, bf16[128,1536]{1,0:T(8,128)(2,1)S(1)}, u32[]{:S(2)}, u32[]{:S(2)}) collective-permute-start(bf16[128,1536]{1,0:T(8,128)(2,1)S(1)} %get-tuple-element.53.refs_0_.refs_2_), channel_id=1, source_target_pairs={{0,12},{1,13},{4,0},{5,1},{8,4},{9,5},{12,8},{13,9},{16,28},{17,29... | collective-permute-start | bytes 1179656 | tf_op jit(solution)/shard_map/ppermute | solution.py:46
  4.3 3.1 %collective-permute-start.2 = (bf16[128,1536]{1,0:T(8,128)(2,1)S(1)}, bf16[128,1536]{1,0:T(8,128)(2,1)S(1)}, u32[]{:S(2)}, u32[]{:S(2)}) collective-permute-start(bf16[128,1536]{1,0:T(8,128)(2,1)S(1)} %get-tuple-element.53.refs_0_.refs_2_), channel_id=1, source_target_pairs={{0,8},{1,9},{4,12},{5,13},{8,0},{9,1},{12,4},{13,5},{16,24},{17,25... | collective-permute-start | bytes 1179656 | tf_op jit(solution)/shard_map/ppermute | solution.py:46
  7.4 3.2 %collective-permute-start.3 = (bf16[128,1536]{1,0:T(8,128)(2,1)S(1)}, bf16[128,1536]{1,0:T(8,128)(2,1)S(1)}, u32[]{:S(2)}, u32[]{:S(2)}) collective-permute-start(bf16[128,1536]{1,0:T(8,128)(2,1)S(1)} %get-tuple-element.52), channel_id=1, source_target_pairs={{0,2},{1,3},{4,6},{5,7},{8,10},{9,11},{12,14},{13,15},{16,18},{17,... | collective-permute-start | bytes 1179656 | tf_op jit(solution)/shard_map/ppermute | solution.py:46
  11.7 10.0 %attention_forward.1 = (bf16[2048,128]{1,0:T(8,128)(2,1)}, f32[2048,128]{1,0:T(8,128)}, bf16[2048,2048]{1,0:T(8,128)(2,1)}) custom-call(bf16[2048,128]{1,0:T(8,128)(2,1)} %bitcast.13, bf16[2048,128]{1,0:T(8,128)(2,1)} %bitcast.15, bf16[2048,128]{1,0:T(8,128)(2,1)} %bitcast.17), custom_call_target="tpu_custom_call" | custom-call | flops 500000000 | bytes 262144 | tf_op jit(solution)/shard_map/attention_forward/pallas_call | solution.py:66
  22.2 5.1 %collective-permute-done.4.other_in = bf16[128,1536]{1,0:T(8,128)(2,1)S(1)} collective-permute-done((bf16[128,1536]{1,0:T(8,128)(2,1)S(1)}, bf16[128,1536]{1,0:T(8,128)(2,1)S(1)}, u32[]{:S(2)}, u32[]{:S(2)}) %collective-permute-start.4) | collective-permute-done | bytes 393248 | tf_op jit(solution)/shard_map/ppermute | solution.py:46
  27.9 2.5 %collective-permute-start.9 = (bf16[2048,128]{1,0:T(8,128)(2,1)}, bf16[2048,128]{1,0:T(8,128)(2,1)S(1)}, u32[]{:S(2)}, u32[]{:S(2)}) collective-permute-start(bf16[2048,128]{1,0:T(8,128)(2,1)} %get-tuple-element.38.refs_0_.refs_3_), channel_id=1, source_target_pairs={{0,2},{1,3},{4,6},{5,7},{8,10},{9,11},{12,14},{13,15},{16,18},{17,... | collective-permute-start | bytes 1572872 | tf_op jit(solution)/shard_map/ppermute | solution.py:46
  32.5 1.8 %collective-permute-start.12 = (bf16[128,1536]{1,0:T(8,128)(2,1)S(1)}, bf16[128,1536]{1,0:T(8,128)(2,1)S(1)}, u32[]{:S(2)}, u32[]{:S(2)}) collective-permute-start(bf16[128,1536]{1,0:T(8,128)(2,1)S(1)} %collective-permute-done.3.refs_2_.refs_0_), channel_id=1, source_target_pairs={{0,4},{1,5},{4,8},{5,9},{8,12},{9,13},{12,0},{13,1},{16,20},{17,21... | collective-permute-start | bytes 1179656 | tf_op jit(solution)/shard_map/ppermute | solution.py:46
  34.9 4.7 %tokens_grad.2 = (bf16[1024,128]{1,0:T(8,128)(2,1)}, bf16[1024,128]{1,0:T(8,128)(2,1)}) custom-call(s32[3]{0:T(128)} %pad_add_fusion.at_ref, bf16[128,3072]{1,0:T(8,128)(2,1)} %own_in.2, bf16[128,1536]{1,0:T(8,128)(2,1)} %copy-done.22, f32[1,3072]{1,0:T(1,128)} %gate_in.3, bf16[128,1536]{1,0:T(8,128)(2,1)} %copy-done.16, bf16[128,1536]{1,0:T(8,128)(2,1)} %copy-done.19, ...), custom_call_target="tpu_custom_call" | custom-call | flops 100000000 | bytes 262144 | tf_op jit(solution)/shard_map/tokens_grad/pallas_call | solution.py:66
  40.7 3.5 %collective-permute-done.9.refs_1_ = bf16[2048,128]{1,0:T(8,128)(2,1)S(1)} collective-permute-done((bf16[2048,128]{1,0:T(8,128)(2,1)}, bf16[2048,128]{1,0:T(8,128)(2,1)S(1)}, u32[]{:S(2)}, u32[]{:S(2)}) %collective-permute-start.9) | collective-permute-done | bytes 524320 | tf_op jit(solution)/shard_map/ppermute | solution.py:46
  45.1 5.2 %projection_grad.2.refs_11_ = f32[256,1536]{1,0:T(8,128)} custom-call(s32[3]{0:T(128)} %pad_add_fusion.at_ref, bf16[2048,128]{1,0:T(8,128)(2,1)} %get-tuple-element.38.refs_0_.refs_3_, bf16[2048,128]{1,0:T(8,128)(2,1)} %copy-done.2, bf16[128,1536]{1,0:T(8,128)(2,1)} %copy-done.16, bf16[128,1536]{1,0:T(8,128)(2,1)} %copy-done.19, ...), custom_call_target="tpu_custom_call" | custom-call | flops 100000000 | bytes 262144 | tf_op jit(solution)/shard_map/projection_grad/pallas_call | solution.py:66
  50.3 1.7 %collective-permute-done.12.refs_8_.refs_6_ = bf16[128,1536]{1,0:T(8,128)(2,1)S(1)} collective-permute-done((bf16[128,1536]{1,0:T(8,128)(2,1)S(1)}, bf16[128,1536]{1,0:T(8,128)(2,1)S(1)}, u32[]{:S(2)}, u32[]{:S(2)}) %collective-permute-start.12) | collective-permute-done | bytes 393248 | tf_op jit(solution)/shard_map/ppermute | solution.py:46
  55.5 1.4 %copy-done = f32[256,1536]{1,0:T(8,128)S(1)} copy-done((f32[256,1536]{1,0:T(8,128)S(1)}, f32[256,1536]{1,0:T(8,128)}, u32[]{:S(2)}) %copy-start) | copy-done | bytes 1572888
  57.9 3.9 %projection_grad.3 = bf16[16,32,768]{2,1,0:T(8,128)(2,1)} custom-call(s32[3]{0:T(128)S(1)} %copy-done.13, bf16[2048,128]{1,0:T(8,128)(2,1)S(1)} %copy-done.1, bf16[2048,128]{1,0:T(8,128)(2,1)S(1)} %copy-done.3, bf16[128,1536]{1,0:T(8,128)(2,1)S(1)} %collective-permute-done.3.refs_2_.refs_0_, bf16[128,1536]{1,0:T(8,128)(2,1)S(1)} %collective-permute-done.14.refs_3_.refs_1_, ...), custom_call_target="tpu_custom_call" | custom-call | flops 100000000 | bytes 262144 | tf_op jit(solution)/shard_map/projection_grad/pallas_call | solution.py:66
  63.4 9.3 %all-to-all-start = ((bf16[16,32,768]{2,1,0:T(8,128)(2,1)}), bf16[16,32,768]{2,1,0:T(8,128)(2,1)S(1)}, u32[]{:S(2)}, u32[]{:S(2)}) async-start(bf16[16,32,768]{2,1,0:T(8,128)(2,1)} %projection_grad.3), calls=%async_computation | async-start | bytes 1572864 | tf_op jit(solution)/shard_map/all_to_all | solution.py:416
  72.8 4.8 %tokens_grad.3 = (bf16[1024,128]{1,0:T(8,128)(2,1)}, bf16[1024,128]{1,0:T(8,128)(2,1)}) custom-call(s32[3]{0:T(128)} %pad_add_fusion.at_ref, bf16[128,3072]{1,0:T(8,128)(2,1)} %own_in.2, bf16[128,1536]{1,0:T(8,128)(2,1)} %copy-done.22, f32[1,3072]{1,0:T(1,128)} %gate_in.3, bf16[128,1536]{1,0:T(8,128)(2,1)} %copy-done.4, bf16[128,1536]{1,0:T(8,128)(2,1)} %copy-done.8, ...), custom_call_target="tpu_custom_call" | custom-call | flops 100000000 | bytes 262144 | tf_op jit(solution)/shard_map/tokens_grad/pallas_call | solution.py:66
  77.6 1.9 %collective-permute-start.18 = (bf16[1024,128]{1,0:T(8,128)(2,1)}, bf16[1024,128]{1,0:T(8,128)(2,1)S(1)}, u32[]{:S(2)}, u32[]{:S(2)}) collective-permute-start(bf16[1024,128]{1,0:T(8,128)(2,1)} %get-tuple-element.45), channel_id=1, source_target_pairs={{0,2},{1,3},{4,6},{5,7},{8,10},{9,11},{12,14},{13,15},{16,18},{17,... | collective-permute-start | bytes 786440 | tf_op jit(solution)/shard_map/ppermute | solution.py:46
  79.5 12.3 %collective-permute-done.18.refs_9_ = bf16[1024,128]{1,0:T(8,128)(2,1)S(1)} collective-permute-done((bf16[1024,128]{1,0:T(8,128)(2,1)}, bf16[1024,128]{1,0:T(8,128)(2,1)S(1)}, u32[]{:S(2)}, u32[]{:S(2)}) %collective-permute-start.18) | collective-permute-done | bytes 262176 | tf_op jit(solution)/shard_map/ppermute | solution.py:46
  91.9 4.4 %all-to-all-done.pieces_ref = bf16[16,32,768]{2,1,0:T(8,128)(2,1)S(1)} async-done(((bf16[16,32,768]{2,1,0:T(8,128)(2,1)}), bf16[16,32,768]{2,1,0:T(8,128)(2,1)S(1)}, u32[]{:S(2)}, u32[]{:S(2)}) %all-to-all-start) | async-done | bytes 786464 | tf_op jit(solution)/shard_map/all_to_all | solution.py:416
  96.3 1.6 %sum_pieces.1 = bf16[32,16,768]{2,1,0:T(8,128)(2,1)} custom-call(s32[3]{0:T(128)S(1)} %copy-done.14, bf16[16,32,768]{2,1,0:T(8,128)(2,1)S(1)} %all-to-all-done.pieces_ref), custom_call_target="tpu_custom_call" | custom-call | flops 10000000 | bytes 262144 | tf_op jit(solution)/shard_map/sum_pieces/pallas_call | solution.py:66
  97.9 7.0 %all-to-all-start.1 = ((bf16[32,16,768]{2,1,0:T(8,128)(2,1)}), bf16[32,16,768]{2,1,0:T(8,128)(2,1)S(1)}, u32[]{:S(2)}, u32[]{:S(2)}) async-start(bf16[32,16,768]{2,1,0:T(8,128)(2,1)} %sum_pieces.1), calls=%async_computation.1 | async-start | bytes 1572864 | tf_op jit(solution)/shard_map/all_to_all | solution.py:430
  104.9 12.7 %attention_backward.1 = (bf16[2048,128]{1,0:T(8,128)(2,1)}, bf16[2048,128]{1,0:T(8,128)(2,1)}, bf16[2048,128]{1,0:T(8,128)(2,1)}) custom-call(s32[3]{0:T(128)} %pad_add_fusion.at_ref, bf16[2048,128]{1,0:T(8,128)(2,1)} %bitcast.14, bf16[2048,128]{1,0:T(8,128)(2,1)} %bitcast.16, bf16[2048,128]{1,0:T(8,128)(2,1)} %bitcast.18, ...), custom_call_target="tpu_custom_call" | custom-call | flops 1000000000 | bytes 262144 | tf_op jit(solution)/shard_map/attention_backward/pallas_call | solution.py:66
  117.6 10.8 %all-to-all-done.1.pieces_ref = bf16[32,16,768]{2,1,0:T(8,128)(2,1)S(1)} async-done(((bf16[32,16,768]{2,1,0:T(8,128)(2,1)}), bf16[32,16,768]{2,1,0:T(8,128)(2,1)S(1)}, u32[]{:S(2)}, u32[]{:S(2)}) %all-to-all-start.1) | async-done | bytes 786464 | tf_op jit(solution)/shard_map/all_to_all | solution.py:430
  128.3 1.2 place_pieces.1
  (77 shorter events, 12.8 us)
Async XLA Ops:
  1.9 33.0 %copy-start.16 = (bf16[128,1536]{1,0:T(8,128)(2,1)}, bf16[128,1536]{1,0:T(8,128)(2,1)S(1)}, u32[]{:S(2)}) copy-start(bf16[128,1536]{1,0:T(8,128)(2,1)S(1)} %get-tuple-element.53.refs_0_.refs_2_) | copy-start | bytes 1179652
  1.9 19.8 %collective-permute-start = (bf16[128,1536]{1,0:T(8,128)(2,1)S(1)}, bf16[128,1536]{1,0:T(8,128)(2,1)S(1)}, u32[]{:S(2)}, u32[]{:S(2)}) collective-permute-start(bf16[128,1536]{1,0:T(8,128)(2,1)S(1)} %get-tuple-element.53.refs_0_.refs_2_), channel_id=1, source_target_pairs={{0,12},{1,13},{4,0},{5,1},{8,4},{9,5},{12,8},{13,9},{16,28},{17,29... | collective-permute-start | bytes 1179656 | tf_op jit(solution)/shard_map/ppermute | solution.py:46
  4.3 17.6 %collective-permute-start.1 = (bf16[128,1536]{1,0:T(8,128)(2,1)S(1)}, bf16[128,1536]{1,0:T(8,128)(2,1)}, u32[]{:S(2)}, u32[]{:S(2)}) collective-permute-start(bf16[128,1536]{1,0:T(8,128)(2,1)S(1)} %get-tuple-element.53.refs_0_.refs_2_), channel_id=1, source_target_pairs={{0,4},{1,5},{4,8},{5,9},{8,12},{9,13},{12,0},{13,1},{16,20},{17,21... | collective-permute-start | bytes 1179656 | tf_op jit(solution)/shard_map/ppermute | solution.py:46
  4.3 17.9 %collective-permute-start.2 = (bf16[128,1536]{1,0:T(8,128)(2,1)S(1)}, bf16[128,1536]{1,0:T(8,128)(2,1)S(1)}, u32[]{:S(2)}, u32[]{:S(2)}) collective-permute-start(bf16[128,1536]{1,0:T(8,128)(2,1)S(1)} %get-tuple-element.53.refs_0_.refs_2_), channel_id=1, source_target_pairs={{0,8},{1,9},{4,12},{5,13},{8,0},{9,1},{12,4},{13,5},{16,24},{17,25... | collective-permute-start | bytes 1179656 | tf_op jit(solution)/shard_map/ppermute | solution.py:46
  7.4 14.9 %collective-permute-start.3 = (bf16[128,1536]{1,0:T(8,128)(2,1)S(1)}, bf16[128,1536]{1,0:T(8,128)(2,1)S(1)}, u32[]{:S(2)}, u32[]{:S(2)}) collective-permute-start(bf16[128,1536]{1,0:T(8,128)(2,1)S(1)} %get-tuple-element.52), channel_id=1, source_target_pairs={{0,2},{1,3},{4,6},{5,7},{8,10},{9,11},{12,14},{13,15},{16,18},{17,... | collective-permute-start | bytes 1179656 | tf_op jit(solution)/shard_map/ppermute | solution.py:46
  10.6 16.7 %collective-permute-start.4 = (bf16[128,1536]{1,0:T(8,128)(2,1)S(1)}, bf16[128,1536]{1,0:T(8,128)(2,1)S(1)}, u32[]{:S(2)}, u32[]{:S(2)}) collective-permute-start(bf16[128,1536]{1,0:T(8,128)(2,1)S(1)} %constant_dynamic-slice_fusion), channel_id=1, source_target_pairs={{0,18},{1,19},{4,22},{5,23},{8,26},{9,27},{12,30},{13,31},{16,2},{... | collective-permute-start | bytes 1179656 | tf_op jit(solution)/shard_map/ppermute | solution.py:46
  21.8 8.6 %collective-permute-start.5 = (bf16[128,1536]{1,0:T(8,128)(2,1)S(1)}, bf16[128,1536]{1,0:T(8,128)(2,1)S(1)}, u32[]{:S(2)}, u32[]{:S(2)}) collective-permute-start(bf16[128,1536]{1,0:T(8,128)(2,1)S(1)} %get-tuple-element.53.refs_0_.refs_2_), channel_id=1, source_target_pairs={{0,1},{1,0},{4,5},{5,4},{8,9},{9,8},{12,13},{13,12},{16,17},{17,16... | collective-permute-start | bytes 1179656 | tf_op jit(solution)/shard_map/ppermute | solution.py:46
  22.2 33.2 %copy-start.4 = (bf16[128,1536]{1,0:T(8,128)(2,1)}, bf16[128,1536]{1,0:T(8,128)(2,1)S(1)}, u32[]{:S(2)}) copy-start(bf16[128,1536]{1,0:T(8,128)(2,1)S(1)} %collective-permute-done.3.refs_2_.refs_0_) | copy-start | bytes 1179652
  27.3 3.4 %collective-permute-start.6 = (bf16[128,1536]{1,0:T(8,128)(2,1)S(1)}, bf16[128,1536]{1,0:T(8,128)(2,1)S(1)}, u32[]{:S(2)}, u32[]{:S(2)}) collective-permute-start(bf16[128,1536]{1,0:T(8,128)(2,1)S(1)} %collective-permute-done.refs_2_.refs_4_), channel_id=1, source_target_pairs={{0,1},{1,0},{4,5},{5,4},{8,9},{9,8},{12,13},{13,12},{16,17},{17,16... | collective-permute-start | bytes 1179656 | tf_op jit(solution)/shard_map/ppermute | solution.py:46
  27.3 4.3 %collective-permute-start.7 = (bf16[128,1536]{1,0:T(8,128)(2,1)S(1)}, bf16[128,1536]{1,0:T(8,128)(2,1)S(1)}, u32[]{:S(2)}, u32[]{:S(2)}) collective-permute-start(bf16[128,1536]{1,0:T(8,128)(2,1)S(1)} %collective-permute-done.2.refs_4_.refs_6_), channel_id=1, source_target_pairs={{0,1},{1,0},{4,5},{5,4},{8,9},{9,8},{12,13},{13,12},{16,17},{17,16... | collective-permute-start | bytes 1179656 | tf_op jit(solution)/shard_map/ppermute | solution.py:46
  27.8 7.1 %collective-permute-start.8 = (bf16[128,1536]{1,0:T(8,128)(2,1)}, bf16[128,1536]{1,0:T(8,128)(2,1)}, u32[]{:S(2)}, u32[]{:S(2)}) collective-permute-start(bf16[128,1536]{1,0:T(8,128)(2,1)} %collective-permute-done.1.refs_6_.refs_8_), channel_id=1, source_target_pairs={{0,1},{1,0},{4,5},{5,4},{8,9},{9,8},{12,13},{13,12},{16,17},{17,16... | collective-permute-start | bytes 1179656 | tf_op jit(solution)/shard_map/ppermute | solution.py:46
  27.9 16.4 %collective-permute-start.9 = (bf16[2048,128]{1,0:T(8,128)(2,1)}, bf16[2048,128]{1,0:T(8,128)(2,1)S(1)}, u32[]{:S(2)}, u32[]{:S(2)}) collective-permute-start(bf16[2048,128]{1,0:T(8,128)(2,1)} %get-tuple-element.38.refs_0_.refs_3_), channel_id=1, source_target_pairs={{0,2},{1,3},{4,6},{5,7},{8,10},{9,11},{12,14},{13,15},{16,18},{17,... | collective-permute-start | bytes 1572872 | tf_op jit(solution)/shard_map/ppermute | solution.py:46
  30.4 19.9 %collective-permute-start.10 = (bf16[128,1536]{1,0:T(8,128)(2,1)S(1)}, bf16[128,1536]{1,0:T(8,128)(2,1)S(1)}, u32[]{:S(2)}, u32[]{:S(2)}) collective-permute-start(bf16[128,1536]{1,0:T(8,128)(2,1)S(1)} %collective-permute-done.3.refs_2_.refs_0_), channel_id=1, source_target_pairs={{0,12},{1,13},{4,0},{5,1},{8,4},{9,5},{12,8},{13,9},{16,28},{17,29... | collective-permute-start | bytes 1179656 | tf_op jit(solution)/shard_map/ppermute | solution.py:46
  30.7 19.6 %collective-permute-start.11 = (bf16[128,1536]{1,0:T(8,128)(2,1)S(1)}, bf16[128,1536]{1,0:T(8,128)(2,1)S(1)}, u32[]{:S(2)}, u32[]{:S(2)}) collective-permute-start(bf16[128,1536]{1,0:T(8,128)(2,1)S(1)} %collective-permute-done.3.refs_2_.refs_0_), channel_id=1, source_target_pairs={{0,8},{1,9},{4,12},{5,13},{8,0},{9,1},{12,4},{13,5},{16,24},{17,25... | collective-permute-start | bytes 1179656 | tf_op jit(solution)/shard_map/ppermute | solution.py:46
  32.5 19.6 %collective-permute-start.12 = (bf16[128,1536]{1,0:T(8,128)(2,1)S(1)}, bf16[128,1536]{1,0:T(8,128)(2,1)S(1)}, u32[]{:S(2)}, u32[]{:S(2)}) collective-permute-start(bf16[128,1536]{1,0:T(8,128)(2,1)S(1)} %collective-permute-done.3.refs_2_.refs_0_), channel_id=1, source_target_pairs={{0,4},{1,5},{4,8},{5,9},{8,12},{9,13},{12,0},{13,1},{16,20},{17,21... | collective-permute-start | bytes 1179656 | tf_op jit(solution)/shard_map/ppermute | solution.py:46
  39.6 12.4 %collective-permute-start.13 = (bf16[1024,128]{1,0:T(8,128)(2,1)}, bf16[1024,128]{1,0:T(8,128)(2,1)}, u32[]{:S(2)}, u32[]{:S(2)}) collective-permute-start(bf16[1024,128]{1,0:T(8,128)(2,1)} %get-tuple-element.39), channel_id=1, source_target_pairs={{0,2},{1,3},{4,6},{5,7},{8,10},{9,11},{12,14},{13,15},{16,18},{17,... | collective-permute-start | bytes 786440 | tf_op jit(solution)/shard_map/ppermute | solution.py:46
  52.1 1.7 %collective-permute-start.14 = (bf16[128,1536]{1,0:T(8,128)(2,1)S(1)}, bf16[128,1536]{1,0:T(8,128)(2,1)S(1)}, u32[]{:S(2)}, u32[]{:S(2)}) collective-permute-start(bf16[128,1536]{1,0:T(8,128)(2,1)S(1)} %collective-permute-done.3.refs_2_.refs_0_), channel_id=1, source_target_pairs={{0,1},{1,0},{4,5},{5,4},{8,9},{9,8},{12,13},{13,12},{16,17},{17,16... | collective-permute-start | bytes 1179656 | tf_op jit(solution)/shard_map/ppermute | solution.py:46
  52.1 2.3 %collective-permute-start.15 = (bf16[128,1536]{1,0:T(8,128)(2,1)S(1)}, bf16[128,1536]{1,0:T(8,128)(2,1)S(1)}, u32[]{:S(2)}, u32[]{:S(2)}) collective-permute-start(bf16[128,1536]{1,0:T(8,128)(2,1)S(1)} %collective-permute-done.10.refs_4_.refs_2_), channel_id=1, source_target_pairs={{0,1},{1,0},{4,5},{5,4},{8,9},{9,8},{12,13},{13,12},{16,17},{17,16... | collective-permute-start | bytes 1179656 | tf_op jit(solution)/shard_map/ppermute | solution.py:46
  52.6 2.3 %collective-permute-start.16 = (bf16[128,1536]{1,0:T(8,128)(2,1)S(1)}, bf16[128,1536]{1,0:T(8,128)(2,1)S(1)}, u32[]{:S(2)}, u32[]{:S(2)}) collective-permute-start(bf16[128,1536]{1,0:T(8,128)(2,1)S(1)} %collective-permute-done.11.refs_6_.refs_4_), channel_id=1, source_target_pairs={{0,1},{1,0},{4,5},{5,4},{8,9},{9,8},{12,13},{13,12},{16,17},{17,16... | collective-permute-start | bytes 1179656 | tf_op jit(solution)/shard_map/ppermute | solution.py:46
  52.7 2.8 %collective-permute-start.17 = (bf16[128,1536]{1,0:T(8,128)(2,1)S(1)}, bf16[128,1536]{1,0:T(8,128)(2,1)S(1)}, u32[]{:S(2)}, u32[]{:S(2)}) collective-permute-start(bf16[128,1536]{1,0:T(8,128)(2,1)S(1)} %collective-permute-done.12.refs_8_.refs_6_), channel_id=1, source_target_pairs={{0,1},{1,0},{4,5},{5,4},{8,9},{9,8},{12,13},{13,12},{16,17},{17,16... | collective-permute-start | bytes 1179656 | tf_op jit(solution)/shard_map/ppermute | solution.py:46
  63.4 32.9 %all-to-all-start = ((bf16[16,32,768]{2,1,0:T(8,128)(2,1)}), bf16[16,32,768]{2,1,0:T(8,128)(2,1)S(1)}, u32[]{:S(2)}, u32[]{:S(2)}) async-start(bf16[16,32,768]{2,1,0:T(8,128)(2,1)} %projection_grad.3), calls=%async_computation | async-start | bytes 1572864 | tf_op jit(solution)/shard_map/all_to_all | solution.py:416
  72.8 23.6 %copy-start.14 = (s32[3]{0:T(128)S(1)}, s32[3]{0:T(128)}, u32[]{:S(2)}) copy-start(s32[3]{0:T(128)} %pad_add_fusion.at_ref) | copy-start | bytes 40
  77.6 14.3 %collective-permute-start.18 = (bf16[1024,128]{1,0:T(8,128)(2,1)}, bf16[1024,128]{1,0:T(8,128)(2,1)S(1)}, u32[]{:S(2)}, u32[]{:S(2)}) collective-permute-start(bf16[1024,128]{1,0:T(8,128)(2,1)} %get-tuple-element.45), channel_id=1, source_target_pairs={{0,2},{1,3},{4,6},{5,7},{8,10},{9,11},{12,14},{13,15},{16,18},{17,... | collective-permute-start | bytes 786440 | tf_op jit(solution)/shard_map/ppermute | solution.py:46
  97.9 30.4 %all-to-all-start.1 = ((bf16[32,16,768]{2,1,0:T(8,128)(2,1)}), bf16[32,16,768]{2,1,0:T(8,128)(2,1)S(1)}, u32[]{:S(2)}, u32[]{:S(2)}) async-start(bf16[32,16,768]{2,1,0:T(8,128)(2,1)} %sum_pieces.1), calls=%async_computation.1 | async-start | bytes 1572864 | tf_op jit(solution)/shard_map/all_to_all | solution.py:430
  (21 other events, 144.4 us)
